TPU v7x, 32 devices: a whole 2x2x4 slice. The times are simulated.
32 devices in a mesh: dp: 4 (over y, core), wide: 8 (over z, x).
Axes of the slice: x: 2, y: 2, z: 4, core: 2. Of those that a mesh axis runs over, the one named last changes fastest.
Arguments:
- tokens: bfloat16 [32768, 768], P(('dp', 'wide')), may hold values from -6 to 6
- lengths: int32 [512], P(('dp', 'wide')), may hold values from 8 to 64
- indices: int32 [512, 10], P(('dp', 'wide')), may hold values from 0 to 8191, as said below
- memory_table: bfloat16 [8192, 3072], P('wide'), may hold values from -6 to 6
- w_query: bfloat16 [768, 768], P('dp'), may hold values from -0.078125 to 0.078125
- w_key: bfloat16 [768, 768], P('dp'), may hold values from -0.21875 to 0.21875
- w_value: bfloat16 [768, 768], P('dp'), may hold values from -0.21875 to 0.21875
- w_out: bfloat16 [768, 768], P('dp'), may hold values from -0.625 to 0.625
- w_in: bfloat16 [768, 3072], P('dp'), may hold values from -0.21875 to 0.21875
- w_back: bfloat16 [3072, 768], P('dp'), may hold values from -0.109375 to 0.109375
- gain_one: bfloat16 [768], P('dp'), may hold values from 0.5 to 1.5
- gain_two: bfloat16 [768], P('dp'), may hold values from 0.5 to 1.5
- rel_bias: bfloat16 [32, 12], P('dp'), may hold values from -4 to 4
- cotangent: bfloat16 [32768, 768], P(('dp', 'wide')), may hold values from -6 to 6
Outputs:
- layer_out: bfloat16 [32768, 768], P(('dp', 'wide'))
- grad_tokens: float32 [32768, 768], P(('dp', 'wide'))
- grad_query: float32 [768, 768], P('dp')
- grad_key: float32 [768, 768], P('dp')
- grad_value: float32 [768, 768], P('dp')
- grad_out: float32 [768, 768], P('dp')
- grad_in: float32 [768, 3072], P('dp')
- grad_back: float32 [3072, 768], P('dp')
- grad_gain_one: float32 [768], P('dp')
- grad_gain_two: float32 [768], P('dp')
- grad_bias: float32 [32, 12], P('dp')
- grad_table: float32 [8192, 3072], P('wide', 'dp')
Inputs may be any that keep to these rules, and one draw needn't show every extreme that they name: `indices`: row n of memory_table is held by index n // 1024 of wide. The 16 questions of one device name at most 21 rows held by any one index of wide, and exactly 21 held by some index; the first, the middle and the last index are named by every device's questions. Rows may repeat.
All inputs are finite; a program needn't handle non-finite values.
Results may differ from a plain program's by a relative error of at most 0.02.
Values may be sent and summed in bfloat16 or wider, within the bound.
No kernel may reach another device: no remote copies, remote signals or barrier semaphores. Data moves between devices by JAX's collectives and lax.ppermute only.
A program may use at most 192 MiB of HBM per device.

v0:
```python
import math

import jax
import jax.numpy as jnp
import numpy as np
from jax import lax
from jax.sharding import PartitionSpec as P

HEADS = 12
HD = 64
NB = 32
MAXDIST = 128
QLEN = 64
TOPK = 10


exact_mode = lax.Precision.HIGHEST


def bucket_table(length, buckets, max_reach):
    half_count = buckets // 2
    near_count = half_count // 2
    onehot = np.zeros((length * length, buckets), np.float32)
    for target in range(length):
        for source in range(length):
            offset = source - target
            bucket = half_count if offset > 0 else 0
            distance = abs(offset)
            if distance < near_count:
                bucket += distance
            else:
                bucket += min(
                    half_count - 1,
                    near_count
                    + int(
                        math.log(distance / near_count)
                        / math.log(max_reach / near_count)
                        * (half_count - near_count)
                    ),
                )
            onehot[target * length + source, bucket] = 1.0
    return onehot


def rms_scale(values, gain_vec):
    return values * lax.rsqrt(jnp.mean(values * values, axis=-1, keepdims=True) + 1e-06) * gain_vec


def soft_masked(scores, key_valid):
    return jax.nn.softmax(jnp.where(key_valid, scores, -1000000000.0), axis=-1)


def matmul_tn(left_side, right_side, mode=None):
    return lax.dot_general(
        left_side,
        right_side,
        (((0,), (0,)), ((), ())),
        precision=mode,
        preferred_element_type=jnp.float32,
    )


def matmul_nt(left_side, right_side):
    return lax.dot_general(
        left_side, right_side, (((1,), (1,)), ((), ())), preferred_element_type=jnp.float32
    )


def slot_rank(owners):
    same_owner = owners[..., :, None] == owners[..., None, :]
    column_ids = jnp.arange(owners.shape[-1])
    earlier = column_ids[None, :] < column_ids[:, None]
    return jnp.sum((same_owner & earlier).astype(jnp.int32), axis=-1)


def shards(
    tokens,
    lengths,
    indices,
    memory_table,
    w_query,
    w_key,
    w_value,
    w_out,
    w_in,
    w_back,
    gain_one,
    gain_two,
    rel_bias,
    cotangent,
):
    (
        full_query,
        full_key,
        full_value,
        full_out,
        full_in,
        full_back,
        full_gain_one,
        full_gain_two,
        full_bias,
    ) = (
        lax.all_gather(w_query, "dp", axis=0, tiled=True),
        lax.all_gather(w_key, "dp", axis=0, tiled=True),
        lax.all_gather(w_value, "dp", axis=0, tiled=True),
        lax.all_gather(w_out, "dp", axis=0, tiled=True),
        lax.all_gather(w_in, "dp", axis=0, tiled=True),
        lax.all_gather(w_back, "dp", axis=0, tiled=True),
        lax.all_gather(gain_one, "dp", axis=0, tiled=True),
        lax.all_gather(gain_two, "dp", axis=0, tiled=True),
        lax.all_gather(rel_bias, "dp", axis=0, tiled=True),
    )
    question_count = lengths.shape[0]
    model_width = tokens.shape[1]
    rows_dev = tokens.shape[0]
    wide_count = lax.axis_size("wide")
    wide_index = lax.axis_index("wide")
    per_dev = question_count * TOPK
    capacity = (per_dev + wide_count - 1) // wide_count + 1
    entries_dev = memory_table.shape[0]
    requests = lax.all_gather(indices, "wide", axis=0, tiled=True).reshape(wide_count, per_dev)
    owner_all = requests // entries_dev
    rank_all = slot_rank(owner_all)
    local_entry = requests - owner_all * entries_dev
    owned_here = owner_all == wide_index
    entry_hot = (
        (local_entry[:, :, None] == jnp.arange(entries_dev)[None, None, :]) & owned_here[:, :, None]
    ).astype(jnp.bfloat16)
    rank_hot = (rank_all[:, :, None] == jnp.arange(capacity)[None, None, :]).astype(jnp.bfloat16)
    selection = (
        jnp.einsum("wrc,wre->wce", rank_hot, entry_hot, preferred_element_type=jnp.float32)
        .astype(jnp.bfloat16)
        .reshape(wide_count * capacity, entries_dev)
    )
    outgoing = (
        jnp.dot(selection, memory_table, preferred_element_type=jnp.float32)
        .astype(jnp.bfloat16)
        .reshape(wide_count, capacity, 4 * model_width)
    )
    incoming = lax.all_to_all(outgoing, "wide", split_axis=0, concat_axis=0, tiled=True)
    own_owner = indices.reshape(per_dev) // entries_dev
    own_slot = own_owner * capacity + slot_rank(own_owner)
    slot_hot = (own_slot[:, None] == jnp.arange(wide_count * capacity)[None, :]).astype(
        jnp.bfloat16
    )
    prefix = (
        jnp.dot(
            slot_hot,
            incoming.reshape(wide_count * capacity, 4 * model_width),
            preferred_element_type=jnp.float32,
        )
        .astype(jnp.bfloat16)
        .reshape(question_count, TOPK, 4, model_width)
    )
    inputs = tokens.astype(jnp.float32)
    normed_full, norm_back_one = jax.vjp(rms_scale, inputs, full_gain_one.astype(jnp.float32))
    normed = normed_full.astype(jnp.bfloat16)
    queries = jnp.dot(normed, full_query, preferred_element_type=jnp.float32).astype(jnp.bfloat16)
    keys = jnp.dot(normed, full_key, preferred_element_type=jnp.float32).astype(jnp.bfloat16)
    values = jnp.dot(normed, full_value, preferred_element_type=jnp.float32).astype(jnp.bfloat16)
    query_heads = queries.reshape(question_count, QLEN, HEADS, HD)
    all_keys = jnp.concatenate(
        [
            prefix[:, :, 0:2].reshape(question_count, 2 * TOPK, HEADS, HD),
            keys.reshape(question_count, QLEN, HEADS, HD),
        ],
        axis=1,
    )
    all_values = jnp.concatenate(
        [
            prefix[:, :, 2:4].reshape(question_count, 2 * TOPK, HEADS, HD),
            values.reshape(question_count, QLEN, HEADS, HD),
        ],
        axis=1,
    )
    onehot = jnp.asarray(bucket_table(QLEN, NB, MAXDIST), jnp.float32)
    position_bias = (
        jnp.dot(onehot, full_bias.astype(jnp.float32), precision=exact_mode)
        .reshape(QLEN, QLEN, HEADS)
        .transpose(2, 0, 1)
    )
    bias_full = jnp.concatenate(
        [jnp.zeros((HEADS, QLEN, 2 * TOPK), jnp.float32), position_bias], axis=2
    )
    scores = (
        jnp.einsum("bihd,bjhd->bhij", query_heads, all_keys, preferred_element_type=jnp.float32)
        + bias_full[None]
    )
    token_valid = jnp.arange(QLEN)[None, :] < lengths[:, None]
    key_valid = jnp.concatenate([jnp.ones((question_count, 2 * TOPK), bool), token_valid], axis=1)[
        :, None, None, :
    ]
    probs, soft_back = jax.vjp(lambda score_set: soft_masked(score_set, key_valid), scores)
    probs_low = probs.astype(jnp.bfloat16)
    context = (
        jnp.einsum("bhij,bjhd->bihd", probs_low, all_values, preferred_element_type=jnp.float32)
        .reshape(rows_dev, model_width)
        .astype(jnp.bfloat16)
    )
    middle = inputs + jnp.dot(context, full_out, preferred_element_type=jnp.float32)
    normed_mid, norm_back_two = jax.vjp(rms_scale, middle, full_gain_two.astype(jnp.float32))
    normed_two = normed_mid.astype(jnp.bfloat16)
    hidden = jnp.dot(normed_two, full_in, preferred_element_type=jnp.float32)
    active_full, gelu_back = jax.vjp(
        lambda hidden_set: jax.nn.gelu(hidden_set, approximate=True), hidden
    )
    active = active_full.astype(jnp.bfloat16)
    layer_out = (middle + jnp.dot(active, full_back, preferred_element_type=jnp.float32)).astype(
        jnp.bfloat16
    )
    upstream = cotangent.astype(jnp.float32)
    grad_back = matmul_tn(active, cotangent)
    grad_active = matmul_nt(cotangent, full_back)
    grad_hidden = gelu_back(grad_active)[0].astype(jnp.bfloat16)
    grad_in = matmul_tn(normed_two, grad_hidden)
    grad_normed_two = matmul_nt(grad_hidden, full_in)
    grad_mid_norm, grad_gain_two = norm_back_two(grad_normed_two)
    grad_middle = upstream + grad_mid_norm
    grad_mid_low = grad_middle.astype(jnp.bfloat16)
    grad_out = matmul_tn(context, grad_mid_low)
    grad_context = (
        matmul_nt(grad_mid_low, full_out)
        .astype(jnp.bfloat16)
        .reshape(question_count, QLEN, HEADS, HD)
    )
    grad_probs = jnp.einsum(
        "bihd,bjhd->bhij", grad_context, all_values, preferred_element_type=jnp.float32
    )
    grad_values_all = jnp.einsum(
        "bhij,bihd->bjhd", probs_low, grad_context, preferred_element_type=jnp.float32
    )
    grad_scores = soft_back(grad_probs)[0].astype(jnp.bfloat16)
    grad_query_heads = jnp.einsum(
        "bhij,bjhd->bihd", grad_scores, all_keys, preferred_element_type=jnp.float32
    )
    grad_keys_all = jnp.einsum(
        "bhij,bihd->bjhd", grad_scores, query_heads, preferred_element_type=jnp.float32
    )
    bias_terms = jnp.sum(grad_scores[..., 2 * TOPK :].astype(jnp.float32), axis=0).reshape(
        HEADS, QLEN * QLEN
    )
    grad_bias = jnp.dot(bias_terms, onehot, precision=exact_mode).T
    grad_queries = grad_query_heads.reshape(rows_dev, model_width).astype(jnp.bfloat16)
    grad_keys = grad_keys_all[:, 2 * TOPK :].reshape(rows_dev, model_width).astype(jnp.bfloat16)
    grad_values = grad_values_all[:, 2 * TOPK :].reshape(rows_dev, model_width).astype(jnp.bfloat16)
    grad_query = matmul_tn(normed, grad_queries)
    grad_key = matmul_tn(normed, grad_keys)
    grad_value = matmul_tn(normed, grad_values)
    grad_normed = (
        matmul_nt(grad_queries, full_query)
        + matmul_nt(grad_keys, full_key)
        + matmul_nt(grad_values, full_value)
    )
    grad_input_norm, grad_gain_one = norm_back_one(grad_normed)
    grad_tokens = grad_middle + grad_input_norm
    grad_prefix = jnp.concatenate(
        [
            grad_keys_all[:, : 2 * TOPK].reshape(question_count, TOPK, 2, model_width),
            grad_values_all[:, : 2 * TOPK].reshape(question_count, TOPK, 2, model_width),
        ],
        axis=2,
    ).reshape(per_dev, 4 * model_width)
    returned = matmul_tn(slot_hot.astype(jnp.float32), grad_prefix, exact_mode).reshape(
        wide_count, capacity, 4 * model_width
    )
    arrived = lax.all_to_all(
        returned.astype(jnp.bfloat16), "wide", split_axis=0, concat_axis=0, tiled=True
    ).astype(returned.dtype)
    grad_table_part = matmul_tn(
        selection.astype(jnp.float32),
        arrived.reshape(wide_count * capacity, 4 * model_width),
        exact_mode,
    )
    reduced = (
        lax.psum_scatter(
            grad_query.astype(jnp.bfloat16), "dp", scatter_dimension=0, tiled=True
        ).astype(jnp.float32),
        lax.psum_scatter(
            grad_key.astype(jnp.bfloat16), "dp", scatter_dimension=0, tiled=True
        ).astype(jnp.float32),
        lax.psum_scatter(
            grad_value.astype(jnp.bfloat16), "dp", scatter_dimension=0, tiled=True
        ).astype(jnp.float32),
        lax.psum_scatter(
            grad_out.astype(jnp.bfloat16), "dp", scatter_dimension=0, tiled=True
        ).astype(jnp.float32),
        lax.psum_scatter(
            grad_in.astype(jnp.bfloat16), "dp", scatter_dimension=0, tiled=True
        ).astype(jnp.float32),
        lax.psum_scatter(
            grad_back.astype(jnp.bfloat16), "dp", scatter_dimension=0, tiled=True
        ).astype(jnp.float32),
        lax.psum_scatter(
            grad_gain_one.astype(jnp.bfloat16), "dp", scatter_dimension=0, tiled=True
        ).astype(jnp.float32),
        lax.psum_scatter(
            grad_gain_two.astype(jnp.bfloat16), "dp", scatter_dimension=0, tiled=True
        ).astype(jnp.float32),
        lax.psum_scatter(
            grad_bias.astype(jnp.bfloat16), "dp", scatter_dimension=0, tiled=True
        ).astype(jnp.float32),
        lax.psum_scatter(
            grad_table_part.astype(jnp.bfloat16), "dp", scatter_dimension=1, tiled=True
        ).astype(jnp.float32),
    )
    totals = (
        lax.psum(reduced[0].astype(jnp.bfloat16), "wide").astype(jnp.float32),
        lax.psum(reduced[1].astype(jnp.bfloat16), "wide").astype(jnp.float32),
        lax.psum(reduced[2].astype(jnp.bfloat16), "wide").astype(jnp.float32),
        lax.psum(reduced[3].astype(jnp.bfloat16), "wide").astype(jnp.float32),
        lax.psum(reduced[4].astype(jnp.bfloat16), "wide").astype(jnp.float32),
        lax.psum(reduced[5].astype(jnp.bfloat16), "wide").astype(jnp.float32),
        lax.psum(reduced[6].astype(jnp.bfloat16), "wide").astype(jnp.float32),
        lax.psum(reduced[7].astype(jnp.bfloat16), "wide").astype(jnp.float32),
        lax.psum(reduced[8].astype(jnp.bfloat16), "wide").astype(jnp.float32),
    )
    table_out = reduced[9]
    bias_out = totals[8]
    return (
        layer_out,
        grad_tokens,
        totals[0],
        totals[1],
        totals[2],
        totals[3],
        totals[4],
        totals[5],
        totals[6],
        totals[7],
        bias_out,
        table_out,
    )


def solution(mesh):
    placed = (
        P(("dp", "wide"), None),
        P(("dp", "wide")),
        P(("dp", "wide"), None),
        P("wide", None),
        P("dp", None),
        P("dp", None),
        P("dp", None),
        P("dp", None),
        P("dp", None),
        P("dp", None),
        P("dp"),
        P("dp"),
        P("dp", None),
        P(("dp", "wide"), None),
    )
    return jax.shard_map(
        shards,
        mesh=mesh,
        in_specs=placed,
        out_specs=(
            P(("dp", "wide"), None),
            P(("dp", "wide"), None),
            P("dp", None),
            P("dp", None),
            P("dp", None),
            P("dp", None),
            P("dp", None),
            P("dp", None),
            P("dp"),
            P("dp"),
            P("dp", None),
            P("wide", "dp"),
        ),
        check_vma=False,
    )
```

profile of v0, /device:TPU:0, one launch (start us, length us, event | category | flops | bytes accessed | tf_op | source)
XLA Modules:
  0.0 680.6 jit_solution(12828474761756299247)
XLA Ops:
  10.6 32.5 %all_gather.30 = s32[128,10]{1,0:T(8,128)S(1)} all-gather(s32[16,10]{1,0:T(8,128)} %param.17), channel_id=1, replica_groups=mesh['dp'=4,'wide'=8] {'wide'}, dimensions={0}, use_global_device_ids=true | all-gather | bytes 5760 | tf_op jit(solution)/shard_map/all_gather | solution.py:121
  46.1 4.1 convolution_convert_fusion.3
  51.6 5.5 all-to-all-start
  60.2 6.1 all-reduce.10
  66.3 5.4 all_gather.35
  81.7 3.9 reshape.348
  85.6 6.5 copy.114
  98.9 6.5 copy.119
  112.1 6.5 copy.128
  137.5 4.5 copy.113
  142.0 4.5 copy.118
  146.5 5.3 fusion.31
  151.8 4.9 fusion.56
  156.7 4.1 convert_bitcast_fusion.1
  160.9 4.2 copy.121
  165.1 4.6 convert_element_type.197
  169.7 5.1 multiply_reduce_fusion.3
  174.9 11.0 %fusion.47 = f32[1024,3072]{1,0:T(8,128)} fusion(bf16[768,3072]{1,0:T(8,128)(2,1)} %all-gather.15.cloned.1.call-done, f32[1024,768]{0,1:T(8,128)} %get-tuple-element.87, f32[768]{0:T(1024)S(1)} %convert_element_type.198, f32[1024]{0:T(1024)S(1)} %fusion.41), kind=kOutput, calls=%fused_computation.116 | convolution fusion | flops 4834197504 | bytes 20454400 | tf_op jit(solution)/shard_map/dot_general | solution.py:203
  186.0 15.7 %fusion.7 = bf16[1024,3072]{1,0:T(8,128)(2,1)S(1)} fusion(f32[1024,3072]{1,0:T(8,128)} %fusion.47, bf16[1024,768]{1,0:T(8,128)(2,1)} %param.28, bf16[3072,768]{1,0:T(8,128)(2,1)} %all-gather.17.cloned.1.call-done), kind=kOutput, calls=%fused_computation.9 | convolution fusion | flops 4894752768 | bytes 25165824 | tf_op jit(solution)/shard_map/dot_general | solution.py:64
  201.7 5.4 multiply_reduce_fusion.1
  215.9 3.9 reshape.359
  219.9 6.8 copy.132
  226.6 8.2 %multiply_reduce_fusion = (f32[16,12,64]{2,1,0:T(8,128)S(1)}, f32[16,12,64,84]{3,2,1,0:T(8,128)S(1)}) fusion(f32[16,12,64,84]{3,2,1,0:T(8,128)} %copy-done.4, f32[16,12,64]{2,1,0:T(8,128)S(1)} %multiply_divide_fusion, bf16[16,64,12,64]{1,3,2,0:T(8,128)(2,1)} %copy.132, bf16[16,64,12,64]{1,3,2,0:T(8,128)(2,1)S(1)} %copy-done.13, ...), kind=kOutput, calls=%fused_computation.16 | convolution fusion | flops 139333632 | bytes 11993088 | tf_op jit(solution)/shard_map/bihd,bjhd->bhij/dot_general | solution.py:226
  234.9 7.8 %select_convert_fusion = bf16[16,12,64,84]{3,2,1,0:T(8,128)(2,1)S(1)} fusion(f32[16,12,64,84]{3,2,1,0:T(8,128)} %copy-done.4, f32[16,12,64,84]{3,2,1,0:T(8,128)S(1)} %get-tuple-element.90, f32[16,12,64]{2,1,0:T(8,128)S(1)} %neg.6, f32[16,12,64]{2,1,0:T(8,128)S(1)} %get-tuple-element.84, pred[16,84]{1,0:T(8,128)(4,1)S(1)} %copy-done.34), kind=kLoop, calls=%fused_computation.15 | loop fusion | flops 5160960 | bytes 10421568 | tf_op jit(solution)/shard_map/convert_element_type | solution.py:232
  244.7 4.2 copy.127
  248.8 5.4 convert_element_type.209
  254.2 4.3 convolution_convert_fusion.12
  264.2 4.2 copy.129
  268.4 5.4 convert_element_type.210
  273.8 4.3 convolution_convert_fusion.11
  278.4 4.9 convolution_bitcast_fusion
  285.9 4.2 copy.133
  290.0 5.4 convert_element_type.211
  295.5 4.6 convolution_convert_fusion.10
  300.1 9.7 %convolution_convert_fusion.1 = bf16[768,3072]{1,0:T(8,128)(2,1)} fusion(bf16[1024,3072]{1,0:T(8,128)(2,1)} %copy-done.43, f32[1024,768]{0,1:T(8,128)} %get-tuple-element.87, f32[768]{0:T(1024)S(1)} %convert_element_type.198, f32[1024]{0:T(1024)S(1)} %fusion.41), kind=kOutput, calls=%fused_computation.29 | convolution fusion | flops 4836556800 | bytes 14162944 | tf_op jit(solution)/shard_map/dot_general | solution.py:54
  309.9 12.1 %convolution_convert_fusion = bf16[3072,768]{1,0:T(8,128)(2,1)} fusion(bf16[1024,768]{1,0:T(8,128)(2,1)} %param.28, f32[1024,3072]{1,0:T(8,128)} %fusion.47), kind=kOutput, calls=%fused_computation.28 | convolution fusion | flops 4862509056 | bytes 18874368 | tf_op jit(solution)/shard_map/dot_general | solution.py:54
  322.1 21.4 %reduce-scatter.13.cloned.1.call-done = bf16[192,768]{1,0:T(8,128)(2,1)} async-done(((bf16[768,768]{1,0:T(8,128)(2,1)}), bf16[192,768]{1,0:T(8,128)(2,1)}) %reduce-scatter.13.cloned.1.call-update) | async-done | bytes 294928 | tf_op jit(solution)/shard_map/reduce_scatter | solution.py:281
  343.6 50.4 %reduce-scatter.17.cloned.1.call-done = bf16[192,3072]{1,0:T(8,128)(2,1)} async-done(((bf16[768,3072]{1,0:T(8,128)(2,1)}), bf16[192,3072]{1,0:T(8,128)(2,1)}) %reduce-scatter.17.cloned.1.call-update) | async-done | bytes 1179664 | tf_op jit(solution)/shard_map/reduce_scatter | solution.py:287
  394.0 50.4 %reduce-scatter.19.cloned.1.call-done = bf16[768,768]{1,0:T(8,128)(2,1)} async-done(((bf16[3072,768]{1,0:T(8,128)(2,1)}), bf16[768,768]{1,0:T(8,128)(2,1)}) %reduce-scatter.19.cloned.1.call-update) | async-done | bytes 1179664 | tf_op jit(solution)/shard_map/reduce_scatter | solution.py:290
  444.7 6.3 copy.136
  453.9 6.8 copy.137
  473.9 47.5 %all_to_all.10 = bf16[8,21,3072]{2,1,0:T(8,128)(2,1)S(1)} all-to-all(bf16[8,21,3072]{2,1,0:T(8,128)(2,1)S(1)} %convolution_convert_fusion.2), channel_id=1, replica_groups=mesh['dp'=4,'wide'=8] {'wide'}, dimensions={0} | all-to-all | bytes 2064384 | tf_op jit(solution)/shard_map/all_to_all | solution.py:266
  521.4 4.5 bitcast_convert_fusion
  527.1 11.7 %add_convert_fusion = bf16[1024,768]{0,1:T(8,128)(2,1)} fusion(f32[1024,768]{0,1:T(8,128)} %get-tuple-element.87, bf16[3072,768]{1,0:T(8,128)(2,1)} %all-gather.17.cloned.1.call-done, f32[1024,3072]{1,0:T(8,128)} %fusion.47), kind=kOutput, calls=%fused_computation.50 | convolution fusion | flops 4861722624 | bytes 22020096 | tf_op jit(solution)/shard_map/dot_general | solution.py:208
  556.0 7.2 %all-reduce.9 = (bf16[32,12]{0,1:T(8,128)(2,1)S(1)}, bf16[768]{0:T(1024)(128)(2,1)S(1)}, bf16[768]{0:T(1024)(128)(2,1)S(1)}) all-reduce(bf16[32,12]{0,1:T(8,128)(2,1)S(1)} %fusion.28, bf16[768]{0:T(1024)(128)(2,1)S(1)} %get-tuple-element.62, bf16[768]{0:T(1024)(128)(2,1)S(1)} %get-tuple-element.60), channel_id=10, replica_groups=mesh['dp'=4,'wide'=8] {'dp'}, use_global_device_ids=true, to_apply=%region_28.29.clone | all-reduce | flops 1920 | bytes 7680
  563.4 20.3 %all-reduce.7 = (bf16[8,12]{0,1:T(8,128)(2,1)S(1)}, bf16[192]{0:T(256)(128)(2,1)S(1)}, bf16[192]{0:T(256)(128)(2,1)S(1)}) all-reduce(bf16[8,12]{0,1:T(8,128)(2,1)S(1)} %constant_dynamic-slice_fusion, bf16[192]{0:T(256)(128)(2,1)S(1)} %dynamic-slice.3, bf16[192]{0:T(256)(128)(2,1)S(1)} %dynamic-slice.5), channel_id=1, replica_groups=mesh['dp'=4,'wide'=8] {'wide'}, use_global_device_ids=true, to_apply=%region_29.30 | all-reduce | flops 480 | bytes 1920 | tf_op jit(solution)/shard_map/psum | solution.py:315
  585.5 25.0 %all-reduce.13.cloned.1.call-done = (bf16[192,768]{1,0:T(8,128)(2,1)}, bf16[192,768]{1,0:T(8,128)(2,1)}, bf16[192,768]{1,0:T(8,128)(2,1)}, bf16[192,768]{1,0:T(8...) async-done(((bf16[192,768]{1,0:T(8,128)(2,1)}, bf16[192,768]{1,0:T(8,128)(2,1)}, bf16[192,768]{1,0:T(8,128)(2,1)}, bf16[192,768]{1,0:T(8,128)(2,1)}, ...) | async-done | bytes 3538960 | tf_op jit(solution)/shard_map/psum | solution.py:307
  621.2 49.1 %reduce-scatter.21.cloned.1.call-done = bf16[1024,768]{1,0:T(8,128)(2,1)} async-done(((bf16[1024,3072]{1,0:T(8,128)(2,1)}), bf16[1024,768]{1,0:T(8,128)(2,1)}) %reduce-scatter.21.cloned.1.call-update) | async-done | bytes 1572880 | tf_op jit(solution)/shard_map/reduce_scatter | solution.py:302
  (206 shorter events, 121.2 us)
Async XLA Ops:
  7.2 71.7 %all-gather.7.cloned.1.call-start = ((), (), s32[]{:S(2)}) async-start(), calls=%async_computation.9 | async-start | bytes 1474560 | tf_op jit(solution)/shard_map/all_gather | solution.py:105
  7.9 84.2 %all-gather.11.cloned.1.call-start = ((), (), s32[]{:S(2)}) async-start(), calls=%async_computation.11 | async-start | bytes 1474560 | tf_op jit(solution)/shard_map/all_gather | solution.py:104
  8.7 96.7 %all-gather.9.cloned.1.call-start = ((), (), s32[]{:S(2)}) async-start(), calls=%async_computation.10 | async-start | bytes 1474560 | tf_op jit(solution)/shard_map/all_gather | solution.py:103
  9.4 160.3 %all-gather.13.cloned.1.call-start = ((), (), s32[]{:S(2)}) async-start(), calls=%async_computation.12 | async-start | bytes 1474560 | tf_op jit(solution)/shard_map/all_gather | solution.py:106
  10.0 165.0 %all-gather.15.cloned.1.call-start = ((), (), s32[]{:S(2)}) async-start(), calls=%async_computation.13 | async-start | bytes 5898240 | tf_op jit(solution)/shard_map/all_gather | solution.py:107
  50.1 7.5 %copy-start.31 = (s32[16,10]{1,0:T(8,128)S(1)}, s32[16,10]{1,0:T(8,128)}, u32[]{:S(2)}) copy-start(s32[16,10]{1,0:T(8,128)} %param.17) | copy-start | bytes 1924
  50.1 7.7 %copy-start.38 = (s32[16]{0:T(128)S(1)}, s32[16]{0:T(128)}, u32[]{:S(2)}) copy-start(s32[16]{0:T(128)} %param.16) | copy-start | bytes 196
  50.1 8.3 %copy-start.37 = (u32[32]{0:T(128)S(1)}, u32[32]{0:T(128)}, u32[]{:S(2)}) copy-start(u32[32]{0:T(128)} %constant.81) | copy-start | bytes 388
  50.2 9.5 %copy-start.41 = (bf16[192]{0:T(256)(128)(2,1)S(1)}, bf16[192]{0:T(256)(128)(2,1)}, u32[]{:S(2)}) copy-start(bf16[192]{0:T(256)(128)(2,1)} %param.25) | copy-start | bytes 1156
  50.2 9.8 %copy-start.42 = (bf16[192]{0:T(256)(128)(2,1)S(1)}, bf16[192]{0:T(256)(128)(2,1)}, u32[]{:S(2)}) copy-start(bf16[192]{0:T(256)(128)(2,1)} %param.26) | copy-start | bytes 1156
  50.2 16.2 %copy-start.36 = (bf16[8,12]{1,0:T(8,128)(2,1)S(1)}, bf16[8,12]{1,0:T(8,128)(2,1)}, u32[]{:S(2)}) copy-start(bf16[8,12]{1,0:T(8,128)(2,1)} %param.27) | copy-start | bytes 580
  50.2 21.5 %copy-start.18 = (f32[4096,32]{0,1:T(8,128)S(1)}, f32[4096,32]{0,1:T(8,128)}, u32[]{:S(2)}) copy-start(f32[4096,32]{0,1:T(8,128)} %constant.72.clone) | copy-start | bytes 1572868
  50.2 22.0 %copy-start.19 = (bf16[1024,768]{1,0:T(8,128)(2,1)S(1)}, bf16[1024,768]{1,0:T(8,128)(2,1)}, u32[]{:S(2)}) copy-start(bf16[1024,768]{1,0:T(8,128)(2,1)} %param.15) | copy-start | bytes 4718596
  51.6 67.0 %all-to-all-start = ((bf16[8,21,3072]{2,1,0:T(8,128)(2,1)}), bf16[8,21,3072]{2,1,0:T(8,128)(2,1)}, u32[]{:S(2)}, u32[]{:S(2)}) async-start(bf16[8,21,3072]{2,1,0:T(8,128)(2,1)} %reshape.322), calls=%async_computation | async-start | bytes 2359296 | tf_op jit(solution)/shard_map/all_to_all | solution.py:140
  57.0 128.9 %all-gather.17.cloned.1.call-start = ((), (), s32[]{:S(2)}) async-start(), calls=%async_computation.14 | async-start | bytes 5898240 | tf_op jit(solution)/shard_map/all_gather | solution.py:108
  57.6 264.5 %reduce-scatter.15.cloned.1.call-start = ((), (), s32[]{:S(2)}) async-start(), calls=%async_computation.18 | async-start | bytes 1474560 | tf_op jit(solution)/shard_map/reduce_scatter | solution.py:284
  73.0 32.4 %copy-start.5 = (bf16[1024,768]{0,1:T(8,128)(2,1)}, bf16[1024,768]{0,1:T(8,128)(2,1)S(1)}, u32[]{:S(2)}) copy-start(bf16[1024,768]{0,1:T(8,128)(2,1)S(1)} %copy.110) | copy-start | bytes 4718596
  73.0 3.2 copy-start.35
  78.3 43.8 %copy-start.32 = (s32[160]{0:T(256)}, s32[160]{0:T(256)S(1)}, u32[]{:S(2)}) copy-start(s32[160]{0:T(256)S(1)} %multiply_add_fusion.3) | copy-start | bytes 1924
  118.6 27.9 %copy-start.1 = (bf16[16,64,12,64]{1,3,2,0:T(8,128)(2,1)}, bf16[16,64,12,64]{1,3,2,0:T(8,128)(2,1)S(1)}, u32[]{:S(2)}) copy-start(bf16[16,64,12,64]{1,3,2,0:T(8,128)(2,1)S(1)} %copy.128) | copy-start | bytes 4718596
  146.5 5.3 copy-start.34
  151.8 4.9 copy-start.12
  151.8 4.9 copy-start.14
  156.7 4.2 copy-start.4
  165.1 4.6 copy-start.6
  169.7 5.2 copy-start.21
  185.9 15.7 %copy-start.9 = (f32[1024,768]{0,1:T(8,128)S(1)}, f32[1024,768]{0,1:T(8,128)}, u32[]{:S(2)}) copy-start(f32[1024,768]{0,1:T(8,128)} %get-tuple-element.87) | copy-start | bytes 9437188
  185.9 15.7 %copy-start.17 = (bf16[768,3072]{1,0:T(8,128)(2,1)S(1)}, bf16[768,3072]{1,0:T(8,128)(2,1)}, u32[]{:S(2)}) copy-start(bf16[768,3072]{1,0:T(8,128)(2,1)} %all-gather.15.cloned.1.call-done) | copy-start | bytes 14155780
  201.6 5.4 copy-start.43
  201.7 5.5 copy-start.16
  209.7 2.9 copy-start.40
  212.1 110.0 %reduce-scatter.9.cloned.1.call-start = ((), (), s32[]{:S(2)}) async-start(), calls=%async_computation.15 | async-start | bytes 1474560 | tf_op jit(solution)/shard_map/reduce_scatter | solution.py:275
  219.9 6.8 copy-start.13
  234.9 7.9 %copy-start.2 = (bf16[16,64,12,64]{1,3,2,0:T(8,128)(2,1)S(1)}, bf16[16,64,12,64]{1,3,2,0:T(8,128)(2,1)}, u32[]{:S(2)}) copy-start(bf16[16,64,12,64]{1,3,2,0:T(8,128)(2,1)} %copy.119) | copy-start | bytes 4718596
  234.9 7.9 %copy-start.3 = (bf16[16,20,12,64]{1,3,2,0:T(8,128)(2,1)S(1)}, bf16[16,20,12,64]{1,3,2,0:T(8,128)(2,1)}, u32[]{:S(2)}) copy-start(bf16[16,20,12,64]{1,3,2,0:T(8,128)(2,1)} %copy.118) | copy-start | bytes 1474564
  258.6 63.5 %reduce-scatter.11.cloned.1.call-start = ((), (), s32[]{:S(2)}) async-start(), calls=%async_computation.16 | async-start | bytes 1474560 | tf_op jit(solution)/shard_map/reduce_scatter | solution.py:278
  261.5 2.7 copy-start
  278.1 65.5 %reduce-scatter.13.cloned.1.call-start = ((), (), s32[]{:S(2)}) async-start(), calls=%async_computation.17 | async-start | bytes 1474560 | tf_op jit(solution)/shard_map/reduce_scatter | solution.py:281
  300.1 93.9 %reduce-scatter.17.cloned.1.call-start = ((), (), s32[]{:S(2)}) async-start(), calls=%async_computation.19 | async-start | bytes 5898240 | tf_op jit(solution)/shard_map/reduce_scatter | solution.py:287
  309.8 134.6 %reduce-scatter.19.cloned.1.call-start = ((), (), s32[]{:S(2)}) async-start(), calls=%async_computation.20 | async-start | bytes 5898240 | tf_op jit(solution)/shard_map/reduce_scatter | solution.py:290
  322.0 288.5 %all-reduce.13.cloned.1.call-start = ((), (), s32[]{:S(2)}) async-start(), calls=%async_computation.22 | async-start | bytes 7077888 | tf_op jit(solution)/shard_map/psum | solution.py:307
  444.5 225.9 %reduce-scatter.21.cloned.1.call-start = ((), (), s32[]{:S(2)}) async-start(), calls=%async_computation.21 | async-start | bytes 7864320 | tf_op jit(solution)/shard_map/reduce_scatter | solution.py:302
  465.3 5.8 copy-start.33
  471.0 50.3 %copy-start.28 = (bf16[8,21,1024]{2,1,0:T(8,128)(2,1)S(1)}, bf16[8,21,1024]{2,1,0:T(8,128)(2,1)}, u32[]{:S(2)}) copy-start(bf16[8,21,1024]{2,1,0:T(8,128)(2,1)} %copy-done.27) | copy-start | bytes 1032196
  543.4 3.4 copy-start.20
  543.4 3.4 copy-start.39
  610.5 7.5 %copy-start.25 = (bf16[192,3072]{1,0:T(8,128)(2,1)S(1)}, bf16[192,3072]{1,0:T(8,128)(2,1)}, u32[]{:S(2)}) copy-start(bf16[192,3072]{1,0:T(8,128)(2,1)} %get-tuple-element.71) | copy-start | bytes 3538948
  612.4 7.2 %copy-start.24 = (bf16[768,768]{1,0:T(8,128)(2,1)S(1)}, bf16[768,768]{1,0:T(8,128)(2,1)}, u32[]{:S(2)}) copy-start(bf16[768,768]{1,0:T(8,128)(2,1)} %get-tuple-element.72) | copy-start | bytes 3538948
  (11 other events, 20.4 us)
Sparse Core Ops, SparseCore 0:
  9.6 20.1 all-gather.6
  31.3 17.4 all-gather.10
  50.4 17.5 all-gather.8
  69.4 17.4 all-gather.12
  88.3 37.4 all-gather.14
  127.2 37.4 all-gather.16
  212.3 27.0 reduce-scatter.14
  258.7 27.0 reduce-scatter.8
  288.9 25.7 reduce-scatter.10
  317.8 25.7 reduce-scatter.12
  346.1 47.8 reduce-scatter.16
  396.6 47.8 reduce-scatter.18
  448.8 161.7 all-reduce.12
  613.1 57.2 reduce-scatter.20
where the time goes:
time: 686 us; the launch traced here: 681 us
  waiting for transfers between devices  200 us (29%)
  local copies, waits for them, and re-layouts  153 us (22%)
  matrix products  150 us (22%)
  blocking collectives  119 us (17%)
  other arithmetic  34.2 us (5%)
  between operations  17.1 us (2%)
    reduce_scatter x1, waiting for transfers between devices, shards(): lax.psum_scatter(grad_in.astype(jnp.bfloat16), 'dp', scatter_dimension=0,...  50.4 us
    reduce_scatter x1, waiting for transfers between devices, shards(): lax.psum_scatter(grad_back.astype(jnp.bfloat16), 'dp', scatter_dimension=...  50.4 us
    reduce_scatter x1, waiting for transfers between devices, shards(): lax.psum_scatter(grad_table_part.astype(jnp.bfloat16), 'dp', scatter_dime...  49.1 us
    all_to_all x1, blocking collectives, shards(): lax.all_to_all(returned.astype(jnp.bfloat16), 'wide', split_axis=0, conca...  47.5 us
    dot_general x8, matrix products, matmul_tn(): lax.dot_general(left_side, right_side, (((0,), (0,)), ((), ())), precisio...  44.8 us
    all_gather x1, blocking collectives, shards(): lax.all_gather(indices, 'wide', axis=0, tiled=True)  32.5 us
    dot_general x6, matrix products, matmul_nt(): lax.dot_general(left_side, right_side, (((1,), (1,)), ((), ())), preferre...  31.3 us
    psum x1, waiting for transfers between devices, shards(): lax.psum(reduced[0].astype(jnp.bfloat16), 'wide').astype(jnp.float32)  25 us
  transfers between devices with their start and end apart: 15, of which 5 were waited for; matrix products, arithmetic and copies ran while one was open for 44% of the time, Pallas kernels for 0%

commit v1 on v0

v1 whole, which is shorter than its diff:
```python
import math

import jax
import jax.numpy as jnp
import numpy as np
from jax import lax
from jax.experimental import pallas as pl
from jax.experimental.pallas import tpu as pltpu
from jax.sharding import PartitionSpec as P

HEADS = 12
HD = 64
NB = 32
MAXDIST = 128
QLEN = 64
TOPK = 10
PADK = 16
LANES = 128
QUAD = 256
EPS = 1e-06
F32 = jnp.float32
BF16 = jnp.bfloat16
VMEM_BYTES = 58 * 1024 * 1024
ANY = pl.BlockSpec(memory_space=pl.ANY)
SMEM = pl.BlockSpec(memory_space=pltpu.SMEM)


def bucket_table(length, buckets, max_reach):
    half_count = buckets // 2
    near_count = half_count // 2
    onehot = np.zeros((length, length, buckets), np.float32)
    for target in range(length):
        for source in range(length):
            offset = source - target
            bucket = half_count if offset > 0 else 0
            distance = abs(offset)
            if distance < near_count:
                bucket += distance
            else:
                bucket += min(
                    half_count - 1,
                    near_count
                    + int(
                        math.log(distance / near_count)
                        / math.log(max_reach / near_count)
                        * (half_count - near_count)
                    ),
                )
            onehot[target, source, bucket] = 1.0
    return onehot


def mm(a, b):
    return jnp.dot(a, b, preferred_element_type=F32)


def mm_nt(a, b):
    return lax.dot_general(a, b, (((1,), (1,)), ((), ())), preferred_element_type=F32)


def mm_tn(a, b):
    return lax.dot_general(a, b, (((0,), (0,)), ((), ())), preferred_element_type=F32)


def cost(flops, size):
    return pl.CostEstimate(flops=int(flops), bytes_accessed=int(size), transcendentals=0)


def params(grid=True):
    return pltpu.CompilerParams(
        vmem_limit_bytes=VMEM_BYTES,
        **(dict(dimension_semantics=("arbitrary",)) if grid else {}),
    )


def rms_factor(values):
    return lax.rsqrt(jnp.mean(values * values, axis=-1, keepdims=True) + EPS)


def block_copies(member, blocks, first, rows, target, sems):
    return [
        pltpu.make_async_copy(
            block.at[pl.ds(first, rows)],
            target.at[pl.ds(pl.multiple_of((member ^ k) * rows, rows), rows)],
            sems.at[k],
        )
        for k, block in enumerate(blocks)
    ]


def qkv_kernel(nd, rows, me, x_ref, gain_ref, *rest):
    blocks, (q_ref, k_ref, v_ref, n_ref, w, sems) = rest[:nd], rest[nd:]

    @pl.when(pl.program_id(0) == 0)
    def _():
        copies = []
        for i in range(3):
            copies += block_copies(me[0], blocks, i * rows, rows, w.at[i], sems.at[i])
        for c in copies:
            c.start()
        for c in copies:
            c.wait()

    x = x_ref[...].astype(F32)
    normed = (x * rms_factor(x) * gain_ref[...]).astype(BF16)
    n_ref[...] = normed
    for i, out in enumerate((q_ref, k_ref, v_ref)):
        out[...] = mm(normed, w[i]).astype(BF16)


def qkv_call(me, x, gain, blocks, rows, tile):
    nd, (count, width) = len(blocks), x.shape
    row_spec = pl.BlockSpec((tile, width), lambda i: (i, 0))
    return pl.pallas_call(
        lambda *refs: qkv_kernel(nd, rows, *refs),
        grid=(count // tile,),
        in_specs=[SMEM, row_spec, pl.BlockSpec((1, width), lambda i: (0, 0))] + [ANY] * nd,
        out_specs=[row_spec] * 4,
        out_shape=[jax.ShapeDtypeStruct((count, width), BF16)] * 4,
        scratch_shapes=[
            pltpu.VMEM((3, width, width), BF16),
            pltpu.SemaphoreType.DMA((3, nd)),
        ],
        compiler_params=params(),
        cost_estimate=cost(6 * count * width * width, 10 * count * width + 6 * width * width),
        name="norm_qkv",
    )(me, x, gain, *blocks)


def key_list(tok, pre, first):
    width = tok.shape[1]
    return jnp.concatenate(
        [
            tok,
            pre[:, first * width : (first + 1) * width],
            pre[:, (first + 1) * width : (first + 2) * width],
            jnp.zeros((LANES - QLEN - 2 * PADK, width), tok.dtype),
        ],
        axis=0,
    )


def spread_heads(part):
    head = lax.broadcasted_iota(jnp.int32, part.shape, 1) // HD
    return jnp.concatenate(
        [jnp.where(head == h, part, jnp.zeros_like(part)) for h in range(QUAD // HD)], axis=0
    )


def gather_heads(full):
    head = lax.broadcasted_iota(jnp.int32, (QLEN, QUAD), 1) // HD
    out = full[:QLEN]
    for h in range(1, QUAD // HD):
        out = jnp.where(head == h, full[h * QLEN : (h + 1) * QLEN], out)
    return out


def attn_kernel(nd, rows, batch, me, lens, *rest):
    (q_ref, k_ref, v_ref, pre_ref, x_ref, bias_ref, gain_ref) = rest[:7]
    blocks = rest[7 : 7 + nd]
    (p_ref, ctx_ref, mid_ref, n2_ref, w, sems) = rest[7 + nd :]
    step = pl.program_id(0)

    @pl.when(step == 0)
    def _():
        copies = block_copies(me[0], blocks, 3 * rows, rows, w, sems)
        for c in copies:
            c.start()
        for c in copies:
            c.wait()

    lane = lax.broadcasted_iota(jnp.int32, (1, LANES), 1)
    fixed = ((lane >= QLEN) & (lane < QLEN + TOPK)) | (
        (lane >= QLEN + PADK) & (lane < QLEN + PADK + TOPK)
    )
    width = q_ref.shape[1]
    for b in range(batch):
        r = slice(b * QLEN, (b + 1) * QLEN)
        pre = pre_ref[b * PADK : (b + 1) * PADK, :]
        keys = key_list(k_ref[r, :], pre, 0)
        values = key_list(v_ref[r, :], pre, 2)
        valid = fixed | (lane < jnp.minimum(lens[step * batch + b], QLEN))
        for t in range(width // QUAD):
            c = slice(t * QUAD, (t + 1) * QUAD)
            scores = mm_nt(spread_heads(q_ref[r, c]), keys[:, c]) + bias_ref[c, :]
            scores = jnp.where(valid, scores, -1e9)
            e = jnp.exp(scores - jnp.max(scores, axis=1, keepdims=True))
            probs = (e * (1.0 / jnp.sum(e, axis=1, keepdims=True))).astype(BF16)
            p_ref[b, c, :] = probs
            ctx_ref[r, c] = gather_heads(mm(probs, values[:, c])).astype(BF16)
    middle = x_ref[...].astype(F32) + mm(ctx_ref[...], w[...])
    mid_ref[...] = middle
    n2_ref[...] = (middle * rms_factor(middle) * gain_ref[...]).astype(BF16)


def attn_call(me, lens, q, k, v, prefix, x, bias, gain, blocks, rows, batch):
    nd, (count, width) = len(blocks), q.shape
    tile = batch * QLEN
    row_spec = pl.BlockSpec((tile, width), lambda i: (i, 0))
    whole = lambda shape: pl.BlockSpec(shape, lambda i: (0,) * len(shape))
    quest = count // QLEN
    return pl.pallas_call(
        lambda *refs: attn_kernel(nd, rows, batch, *refs),
        grid=(count // tile,),
        in_specs=[SMEM, SMEM, row_spec, row_spec, row_spec]
        + [
            pl.BlockSpec((batch * PADK, prefix.shape[1]), lambda i: (i, 0)),
            row_spec,
            whole(bias.shape),
            whole((1, width)),
        ]
        + [ANY] * nd,
        out_specs=[
            pl.BlockSpec((batch, HEADS * QLEN, LANES), lambda i: (i, 0, 0)),
            row_spec,
            row_spec,
            row_spec,
        ],
        out_shape=[
            jax.ShapeDtypeStruct((quest, HEADS * QLEN, LANES), BF16),
            jax.ShapeDtypeStruct((count, width), BF16),
            jax.ShapeDtypeStruct((count, width), F32),
            jax.ShapeDtypeStruct((count, width), BF16),
        ],
        scratch_shapes=[pltpu.VMEM((width, width), BF16), pltpu.SemaphoreType.DMA((nd,))],
        compiler_params=params(),
        cost_estimate=cost(12 * count * width * width, 20 * count * width),
        name="attention",
    )(me, lens, q, k, v, prefix, x, bias, gain, *blocks)


def ff_kernel(nd, rows, tile, me, n2_ref, mid_ref, g_ref, *rest):
    in_blocks, back_blocks = rest[:nd], rest[nd : 2 * nd]
    (out_ref, dn2_ref, bt_ref, bm_ref, it_ref, im_ref) = rest[2 * nd : 2 * nd + 6]
    (win, wback, act, gh, gin, total, in_sems, back_sems) = rest[2 * nd + 6 :]
    step = pl.program_id(0)
    half = nd // 2
    member = me[0]
    count, width = n2_ref.shape
    chunk = wback.shape[1]
    order = [2 * s + 1 for s in range(half)] + [2 * s for s in range(half)]
    rel = jnp.where(step < half, 2 * step + 1, 2 * (step - half))

    @pl.when(step == 0)
    def _():
        copies = block_copies(member, in_blocks, 0, rows, win, in_sems)
        for c in copies:
            c.start()
        for s, k in enumerate(order):
            c = pltpu.make_async_copy(back_blocks[k], wback.at[s], back_sems.at[s])
            c.start()
            copies.append(c)
        for c in copies:
            c.wait()

    cols = pl.ds(pl.multiple_of((member ^ rel) * chunk, LANES), chunk)
    w_in = win[:, cols]
    w_back = wback[step]

    def row_tile(m, carry):
        r = pl.ds(pl.multiple_of(m * tile, tile), tile)
        h = mm(n2_ref[r, :], w_in)
        h2 = h * h
        th = jnp.tanh(math.sqrt(2 / math.pi) * h * (1.0 + 0.044715 * h2))
        a = (0.5 * h * (1.0 + th)).astype(BF16)
        slope = 0.5 * (1.0 + th) + 0.5 * h * (1.0 - th * th) * (
            math.sqrt(2 / math.pi) * (1.0 + 3 * 0.044715 * h2)
        )
        act[r, :] = a
        y = mm(a, w_back)
        d = (mm_nt(g_ref[r, :], w_back) * slope).astype(BF16)
        gh[r, :] = d
        dn = mm_nt(d, w_in)

        @pl.when(step == 0)
        def _():
            total[r, :] = mid_ref[r, :] + y
            dn2_ref[r, :] = dn

        @pl.when(step > 0)
        def _():
            total[r, :] += y
            dn2_ref[r, :] += dn

        return carry

    lax.fori_loop(0, count // tile, row_tile, 0)

    @pl.when(step < half)
    def _():
        bt_ref[...] = mm_tn(act[...], g_ref[...]).astype(BF16)[None]

    @pl.when(step >= half)
    def _():
        bm_ref[...] = mm_tn(act[...], g_ref[...]).astype(BF16)[None]

    gin[:, cols] = mm_tn(n2_ref[...], gh[...]).astype(BF16)

    @pl.when(step == nd - 1)
    def _():
        out_ref[...] = total[...].astype(BF16)
        for kk in range(half):
            for ref, k in ((it_ref, 2 * kk + 1), (im_ref, 2 * kk)):
                ref[kk] = gin[pl.ds(pl.multiple_of((member ^ k) * rows, rows), rows), :]


def ff_call(me, n2, mid, g, in_blocks, back_blocks, tile):
    nd, (count, width) = len(in_blocks), n2.shape
    half = nd // 2
    rows, hidden = in_blocks[0].shape
    chunk = back_blocks[0].shape[0]
    whole = lambda *shape: pl.BlockSpec(shape, lambda i: (0,) * len(shape))
    return pl.pallas_call(
        lambda *refs: ff_kernel(nd, rows, tile, *refs),
        grid=(nd,),
        in_specs=[SMEM] + [whole(count, width)] * 3 + [ANY] * (2 * nd),
        out_specs=[
            whole(count, width),
            whole(count, width),
            pl.BlockSpec((1, chunk, width), lambda i: (jnp.minimum(i, half - 1), 0, 0)),
            pl.BlockSpec((1, chunk, width), lambda i: (jnp.maximum(i - half, 0), 0, 0)),
            whole(half, rows, hidden),
            whole(half, rows, hidden),
        ],
        out_shape=[
            jax.ShapeDtypeStruct((count, width), BF16),
            jax.ShapeDtypeStruct((count, width), F32),
            jax.ShapeDtypeStruct((half, chunk, width), BF16),
            jax.ShapeDtypeStruct((half, chunk, width), BF16),
            jax.ShapeDtypeStruct((half, rows, hidden), BF16),
            jax.ShapeDtypeStruct((half, rows, hidden), BF16),
        ],
        scratch_shapes=[
            pltpu.VMEM((width, hidden), BF16),
            pltpu.VMEM((nd, chunk, width), BF16),
            pltpu.VMEM((count, chunk), BF16),
            pltpu.VMEM((count, chunk), BF16),
            pltpu.VMEM((width, hidden), BF16),
            pltpu.VMEM((count, width), F32),
            pltpu.SemaphoreType.DMA((nd,)),
            pltpu.SemaphoreType.DMA((nd,)),
        ],
        compiler_params=params(),
        cost_estimate=cost(12 * count * width * hidden, 16 * count * width + 8 * width * hidden),
        name="feed_forward",
    )(me, n2, mid, g, *in_blocks, *back_blocks)


def attn_back_kernel(nd, rows, batch, me, *rest):
    (g_ref, dn2_ref, mid_ref, gain_ref, p_ref, q_ref, k_ref, v_ref, pre_ref) = rest[:9]
    blocks = rest[9 : 9 + nd]
    (gm_ref, gml_ref, dq_ref, dk_ref, dv_ref, dpre_ref, dbias_ref, dgain_ref) = rest[9 + nd : 17 + nd]
    w, sems = rest[17 + nd :]
    step = pl.program_id(0)

    @pl.when(step == 0)
    def _():
        copies = block_copies(me[0], blocks, 3 * rows, rows, w, sems)
        for c in copies:
            c.start()
        dbias_ref[...] = jnp.zeros_like(dbias_ref)
        dgain_ref[...] = jnp.zeros_like(dgain_ref)
        for c in copies:
            c.wait()

    mid, dn2 = mid_ref[...], dn2_ref[...]
    r2 = rms_factor(mid)
    scaled = dn2 * gain_ref[...]
    dgain_ref[...] += jnp.sum(dn2 * mid * r2, axis=0, keepdims=True)
    gm = (
        g_ref[...].astype(F32)
        + r2 * scaled
        - mid * (r2 * r2 * r2 * jnp.mean(scaled * mid, axis=-1, keepdims=True))
    )
    gm_ref[...] = gm
    low = gm.astype(BF16)
    gml_ref[...] = low
    dctx = mm_nt(low, w[...]).astype(BF16)
    width = q_ref.shape[1]
    for b in range(batch):
        r = slice(b * QLEN, (b + 1) * QLEN)
        pr = slice(b * PADK, (b + 1) * PADK)
        pre = pre_ref[pr, :]
        keys = key_list(k_ref[r, :], pre, 0)
        values = key_list(v_ref[r, :], pre, 2)
        for t in range(width // QUAD):
            c = slice(t * QUAD, (t + 1) * QUAD)
            gs = spread_heads(dctx[r, c])
            qs = spread_heads(q_ref[r, c])
            low_probs = p_ref[b, c, :]
            probs = low_probs.astype(F32)
            gp = mm_nt(gs, values[:, c])
            dval = mm_tn(low_probs, gs)
            ds = (probs * (gp - jnp.sum(probs * gp, axis=1, keepdims=True))).astype(BF16)
            dbias_ref[c, :] += ds.astype(F32)
            dq_ref[r, c] = gather_heads(mm(ds, keys[:, c])).astype(BF16)
            dkey = mm_tn(ds, qs)
            for ref, first, grad in ((dk_ref, 0, dkey), (dv_ref, 2, dval)):
                low_grad = grad.astype(BF16)
                ref[r, c] = low_grad[:QLEN]
                for s in range(2):
                    at = (first + s) * width + t * QUAD
                    dpre_ref[pr, at : at + QUAD] = low_grad[
                        QLEN + s * PADK : QLEN + (s + 1) * PADK
                    ]


def attn_back_call(me, g, dn2, mid, gain, probs, q, k, v, prefix, blocks, rows, batch):
    nd, (count, width) = len(blocks), q.shape
    tile = batch * QLEN
    row_spec = pl.BlockSpec((tile, width), lambda i: (i, 0))
    pre_spec = pl.BlockSpec((batch * PADK, prefix.shape[1]), lambda i: (i, 0))
    whole = lambda *shape: pl.BlockSpec(shape, lambda i: (0,) * len(shape))
    rows_of = lambda dtype: jax.ShapeDtypeStruct((count, width), dtype)
    return pl.pallas_call(
        lambda *refs: attn_back_kernel(nd, rows, batch, *refs),
        grid=(count // tile,),
        in_specs=[SMEM, row_spec, row_spec, row_spec, whole(1, width)]
        + [pl.BlockSpec((batch, HEADS * QLEN, LANES), lambda i: (i, 0, 0))]
        + [row_spec] * 3
        + [pre_spec]
        + [ANY] * nd,
        out_specs=[row_spec] * 5 + [pre_spec, whole(HEADS * QLEN, LANES), whole(1, width)],
        out_shape=[rows_of(F32)]
        + [rows_of(BF16)] * 4
        + [
            jax.ShapeDtypeStruct(prefix.shape, BF16),
            jax.ShapeDtypeStruct((HEADS * QLEN, LANES), F32),
            jax.ShapeDtypeStruct((1, width), F32),
        ],
        scratch_shapes=[pltpu.VMEM((width, width), BF16), pltpu.SemaphoreType.DMA((nd,))],
        compiler_params=params(),
        cost_estimate=cost(20 * count * width * width, 30 * count * width),
        name="attention_back",
    )(me, g, dn2, mid, gain, probs, q, k, v, prefix, *blocks)


def square_kernel(nd, rows, me, n_ref, ctx_ref, dq_ref, dk_ref, dv_ref, gml_ref, their, mine, full):
    width = n_ref.shape[1]
    for i, (left, right) in enumerate(
        ((n_ref, dq_ref), (n_ref, dk_ref), (n_ref, dv_ref), (ctx_ref, gml_ref))
    ):
        for c in range(0, width, QUAD):
            full[i, c : c + QUAD, :] = mm_tn(left[:, c : c + QUAD], right[...]).astype(BF16)
        for kk in range(nd // 2):
            for ref, k in ((their, 2 * kk + 1), (mine, 2 * kk)):
                at = pl.ds(pl.multiple_of((me[0] ^ k) * rows, rows), rows)
                ref[kk, i * rows : (i + 1) * rows, :] = full[i, at, :]


def square_call(me, nd, rows, normed, ctx, dq, dk, dv, gml):
    count, width = normed.shape
    vmem = pl.BlockSpec(memory_space=pltpu.VMEM)
    shape = jax.ShapeDtypeStruct((nd // 2, 4 * rows, width), BF16)
    return pl.pallas_call(
        lambda *refs: square_kernel(nd, rows, *refs),
        in_specs=[SMEM] + [vmem] * 6,
        out_specs=[vmem] * 2,
        out_shape=[shape] * 2,
        scratch_shapes=[pltpu.VMEM((4, width, width), BF16)],
        compiler_params=params(False),
        cost_estimate=cost(8 * count * width * width, 12 * count * width + 8 * width * width),
        name="square_grads",
    )(me, normed, ctx, dq, dk, dv, gml)


def input_kernel(nd, rows, me, x_ref, gain_ref, gm_ref, dq_ref, dk_ref, dv_ref, *rest):
    blocks, (gt_ref, dgain_ref, w, sems) = rest[:nd], rest[nd:]

    @pl.when(pl.program_id(0) == 0)
    def _():
        copies = []
        for i in range(3):
            copies += block_copies(me[0], blocks, i * rows, rows, w.at[i], sems.at[i])
        for c in copies:
            c.start()
        dgain_ref[...] = jnp.zeros_like(dgain_ref)
        for c in copies:
            c.wait()

    dn = mm_nt(dq_ref[...], w[0]) + mm_nt(dk_ref[...], w[1]) + mm_nt(dv_ref[...], w[2])
    x = x_ref[...].astype(F32)
    r1 = rms_factor(x)
    scaled = dn * gain_ref[...]
    dgain_ref[...] += jnp.sum(dn * x * r1, axis=0, keepdims=True)
    gt_ref[...] = (
        gm_ref[...]
        + r1 * scaled
        - x * (r1 * r1 * r1 * jnp.mean(scaled * x, axis=-1, keepdims=True))
    )


def input_call(me, x, gain, gm, dq, dk, dv, blocks, rows, tile):
    nd, (count, width) = len(blocks), x.shape
    row_spec = pl.BlockSpec((tile, width), lambda i: (i, 0))
    whole = lambda *shape: pl.BlockSpec(shape, lambda i: (0,) * len(shape))
    return pl.pallas_call(
        lambda *refs: input_kernel(nd, rows, *refs),
        grid=(count // tile,),
        in_specs=[SMEM, row_spec, whole(1, width)] + [row_spec] * 4 + [ANY] * nd,
        out_specs=[row_spec, whole(1, width)],
        out_shape=[
            jax.ShapeDtypeStruct((count, width), F32),
            jax.ShapeDtypeStruct((1, width), F32),
        ],
        scratch_shapes=[
            pltpu.VMEM((3, width, width), BF16),
            pltpu.SemaphoreType.DMA((3, nd)),
        ],
        compiler_params=params(),
        cost_estimate=cost(6 * count * width * width, 16 * count * width + 6 * width * width),
        name="input_grad",
    )(me, x, gain, gm, dq, dk, dv, *blocks)


def after(value, *earlier):
    return lax.optimization_barrier((value, *earlier))[0]


class Moves:
    def __init__(self, nd, nw):
        self.nd, self.nw = nd, nw
        self.yn = nd // 2
        self.xn = self.yn if nw % self.yn == 0 else 1
        self.zn = nw // self.xn

    def send(self, value, axis, k):
        if axis in ("core", "y"):
            flip = k if axis == "core" else 2 * k
            return lax.ppermute(value, "dp", [(i, i ^ flip) for i in range(self.nd)])
        flip = k if axis == "x" else self.xn * k
        return lax.ppermute(value, "wide", [(i, i ^ flip) for i in range(self.nw)])

    def where(self, axis):
        if axis == "y":
            return lax.axis_index("dp") // 2
        if axis == "x":
            return lax.axis_index("wide") % self.xn
        return lax.axis_index("wide") // self.xn


def by_distance(parts, place):
    parts = list(parts)
    bit = 1
    while bit < len(parts):
        on = (place & bit) != 0
        parts = [jnp.where(on, parts[i ^ bit], parts[i]) for i in range(len(parts))]
        bit *= 2
    return parts


def cut(value, count, axis):
    size = value.shape[axis] // count
    return [lax.slice_in_dim(value, i * size, (i + 1) * size, axis=axis) for i in range(count)]


def summed(values):
    total = values[0].astype(F32)
    for v in values[1:]:
        total = total + v.astype(F32)
    return total


def scatter_dp(moves, their, mine):
    got = moves.send(their, "core", 1)
    parts = [mine[0], got[0]]
    for kk in range(1, moves.yn):
        parts.append(moves.send(summed([mine[kk], got[kk]]).astype(BF16), "y", kk))
    return summed(parts)


def sum_wide(moves, part):
    px, pz = moves.where("x"), moves.where("z")
    cols = by_distance(cut(part, moves.xn, 1), px)
    kept = [cols[0]] + [moves.send(cols[k].astype(BF16), "x", k) for k in range(1, moves.xn)]
    rows = by_distance(cut(summed(kept), moves.zn, 0), pz)
    kept = [rows[0]] + [moves.send(rows[k].astype(BF16), "z", k) for k in range(1, moves.zn)]
    block = summed(kept).astype(BF16)
    rows = [block] + [moves.send(block, "z", k) for k in range(1, moves.zn)]
    strip = jnp.concatenate(by_distance(rows, pz), axis=0)
    cols = [strip] + [moves.send(strip, "x", k) for k in range(1, moves.xn)]
    return jnp.concatenate(by_distance(cols, px), axis=1).astype(F32)


def gather_dp(moves, shard, earlier=None):
    out = []
    for kk in range(moves.yn):
        far = shard if kk == 0 else moves.send(shard, "y", kk)
        out += [far, moves.send(far, "core", 1)]
    return out


def gather_dp_halves(moves, shard, earlier):
    if moves.yn != 2 or moves.xn != 2:
        return gather_dp(moves, shard)
    px = moves.where("x")
    half = by_distance(cut(shard, 2, 0), px)[0]
    near = moves.send(after(half, earlier), "y", 1)
    far = moves.send(near, "x", 1)
    other = jnp.concatenate(by_distance([near, far], px), axis=0)
    return [shard, moves.send(shard, "core", 1), other, moves.send(other, "core", 1)]


def slot_rank(owners):
    same_owner = owners[:, None] == owners[None, :]
    ids = jnp.arange(owners.shape[0])
    return jnp.sum((same_owner & (ids[None, :] < ids[:, None])).astype(jnp.int32), axis=1)


def shards(
    tokens,
    lengths,
    indices,
    memory_table,
    w_query,
    w_key,
    w_value,
    w_out,
    w_in,
    w_back,
    gain_one,
    gain_two,
    rel_bias,
    cotangent,
):
    nd, nw = lax.axis_size("dp"), lax.axis_size("wide")
    moves = Moves(nd, nw)
    dp_index = lax.axis_index("dp")
    me = dp_index.astype(jnp.int32).reshape(1)
    quest = lengths.shape[0]
    count, width = tokens.shape
    rows = w_query.shape[0]
    entries = memory_table.shape[0]
    per_dev = quest * TOPK
    capacity = (per_dev + nw - 1) // nw + 1
    slots = nw * capacity

    flat = indices.reshape(per_dev)
    owner = flat // entries
    rank = slot_rank(owner)
    local = flat - owner * entries
    hit = (owner[None, None, :] == jnp.arange(nw)[:, None, None]) & (
        rank[None, None, :] == jnp.arange(LANES)[None, :, None]
    )
    request = jnp.sum(jnp.where(hit, local[None, None, :] + 1, 0), axis=2) - 1
    asked = lax.all_to_all(request, "wide", 0, 0, tiled=True)
    asked = asked[:, :capacity].reshape(slots)

    small = jnp.concatenate(
        [gain_one, gain_two, rel_bias.reshape(-1)]
    )
    small = jnp.pad(small, (0, 16 * width - small.shape[0])).reshape(16, width)
    packed = jnp.concatenate([w_query, w_key, w_value, w_out, small], axis=0)
    square = gather_dp(moves, packed)
    ins = gather_dp_halves(moves, w_in, square[2])
    backs = gather_dp_halves(moves, w_back, ins[2])

    selection = (asked[:, None] == jnp.arange(entries)[None, :]).astype(BF16)
    outgoing = jnp.dot(selection, memory_table, preferred_element_type=F32).astype(BF16)
    incoming = lax.all_to_all(
        outgoing.reshape(nw, capacity, 4 * width), "wide", 0, 0, tiled=True
    ).reshape(slots, 4 * width)
    slot = (owner * capacity + rank).reshape(quest, TOPK)
    slot = jnp.pad(slot, ((0, 0), (0, PADK - TOPK)), constant_values=-1).reshape(quest * PADK)
    slot_hot = (slot[:, None] == jnp.arange(slots)[None, :]).astype(BF16)
    prefix = jnp.dot(slot_hot, incoming, preferred_element_type=F32).astype(BF16)

    rows_asked = asked
    rows_asked = jnp.stack([rows_asked, moves.send(rows_asked, "core", 1)])
    rows_asked = jnp.stack(
        [rows_asked] + [moves.send(rows_asked, "y", kk) for kk in range(1, moves.yn)]
    ).reshape(nd * slots)

    smalls = jnp.stack([block[4 * rows :].reshape(-1) for block in square])
    smalls = jnp.take(smalls, jnp.arange(nd) ^ dp_index, axis=0).astype(F32)
    full_gain_one = smalls[:, :rows].reshape(1, width)
    full_gain_two = smalls[:, rows : 2 * rows].reshape(1, width)
    bias_size = rel_bias.size
    full_bias = smalls[:, 2 * rows : 2 * rows + bias_size].reshape(NB, HEADS)
    onehot = np.zeros((QLEN, LANES, NB), np.float32)
    onehot[:, :QLEN] = bucket_table(QLEN, NB, MAXDIST)
    onehot = onehot.reshape(QLEN * LANES, NB)
    bias = jnp.dot(
        full_bias.T.astype(BF16), jnp.asarray(onehot.T, BF16), preferred_element_type=F32
    ).reshape(HEADS * QLEN, LANES)

    tile = 4 * QLEN
    q, k, v, normed = qkv_call(me, tokens, full_gain_one, square, rows, tile)
    probs, ctx, mid, n2 = attn_call(
        me, lengths, q, k, v, prefix, tokens, bias, full_gain_two, square, rows, 4
    )
    layer_out, dn2, back_their, back_mine, in_their, in_mine = ff_call(
        me, n2, mid, cotangent, ins, backs, tile
    )
    grad_back = sum_wide(moves, scatter_dp(moves, back_their, back_mine))
    grad_in = sum_wide(moves, scatter_dp(moves, in_their, in_mine))

    gm, gml, dq, dk, dv, dpre, dbias, dgain_two = attn_back_call(
        me, cotangent, dn2, mid, full_gain_two, probs, q, k, v, prefix, square, rows, 4
    )
    sq_their, sq_mine = square_call(me, nd, rows, normed, ctx, dq, dk, dv, gml)
    grad_square = sum_wide(moves, scatter_dp(moves, sq_their, sq_mine))

    returned = mm_tn(slot_hot, dpre).astype(BF16)
    arrived = lax.all_to_all(
        returned.reshape(nw, capacity, 4 * width), "wide", 0, 0, tiled=True
    ).reshape(slots, nd, 4 * width // nd)
    cols = by_distance([arrived[:, j] for j in range(nd)], dp_index)
    got = moves.send(jnp.stack(cols[1::2]), "core", 1)
    pairs = [jnp.concatenate([cols[2 * kk], got[kk]], axis=0) for kk in range(moves.yn)]
    table_rows = jnp.concatenate(
        [pairs[0]] + [moves.send(pairs[kk], "y", kk) for kk in range(1, moves.yn)], axis=0
    )
    scatter = (jnp.arange(entries)[:, None] == rows_asked[None, :]).astype(BF16)
    grad_table = jnp.dot(scatter, table_rows, preferred_element_type=F32)

    grad_tokens, dgain_one = input_call(
        me, tokens, full_gain_one, gm, dq, dk, dv, square, rows, tile
    )
    bucket_sums = jnp.dot(
        jnp.asarray(onehot.T), dbias.reshape(HEADS, QLEN * LANES).T, precision=lax.Precision.HIGHEST
    )
    small_sums = lax.psum(
        jnp.concatenate([dgain_one[0], dgain_two[0], bucket_sums.reshape(-1)]), ("dp", "wide")
    )
    own = lambda vec, size: lax.dynamic_slice_in_dim(vec, dp_index * size, size)
    grad_gain_one = own(small_sums[:width], rows)
    grad_gain_two = own(small_sums[width : 2 * width], rows)
    grad_bias = own(small_sums[2 * width :].reshape(NB, HEADS), NB // nd)
    return (
        layer_out,
        grad_tokens,
        grad_square[:rows],
        grad_square[rows : 2 * rows],
        grad_square[2 * rows : 3 * rows],
        grad_square[3 * rows :],
        grad_in,
        grad_back,
        grad_gain_one,
        grad_gain_two,
        grad_bias,
        grad_table,
    )


def solution(mesh):
    split = P(("dp", "wide"), None)
    weight = P("dp", None)
    return jax.shard_map(
        shards,
        mesh=mesh,
        in_specs=(split, P(("dp", "wide")), split, P("wide", None))
        + (weight,) * 6
        + (P("dp"), P("dp"), weight, split),
        out_specs=(split, split) + (weight,) * 6 + (P("dp"), P("dp"), weight, P("wide", "dp")),
        check_vma=False,
    )
```

time: 686 us -> 496 us (0.72)
  matrix products: 150 us -> 12.3 us
  local copies, waits for them, and re-layouts: 153 us -> 18.7 us
  Pallas kernels: 0 us -> 122 us
  starting transfers between devices: 6.8 us -> 101 us
  blocking collectives: 119 us -> 40.6 us
  waiting for transfers between devices: 200 us -> 163 us
  between operations: 17.1 us -> 1.94 us
    reduce_scatter x7 -> x0, waiting for transfers between devices: 171 us -> none  [the longest x1 50.4 us: shards(): lax.psum_scatter(grad_in.astype(jnp.bfloat16), 'dp', scatter_dimension=0,...]
    ppermute x0 -> x45, waiting for transfers between devices: none -> 162 us  [the longest x19 106 us: send(): return lax.ppermute(value, 'dp', [(i, i ^ flip) for i in range(self.nd)])]
    dot_general x31 -> x6, matrix products: 150 us -> 12.3 us  [the longest x1 4.06 us: shards(): jnp.dot(selection, memory_table, preferred_element_type=F32).astype(BF16)]
    pallas_call x0 -> x6, Pallas kernels: none -> 122 us  [the longest x1 52.5 us: ff_call(): pl.pallas_call(lambda *refs: ff_kernel(nd, rows, tile, *refs), grid=(nd,)...]
    ppermute x0 -> x45, starting transfers between devices: none -> 83.2 us  [the longest x26 69.5 us: send(): return lax.ppermute(value, 'wide', [(i, i ^ flip) for i in range(self.nw)])]
    reshape x23 -> x13, local copies, waits for them, and re-layouts: 75.3 us -> 7.71 us  [the longest x1 1.35 us: shards(): outgoing.reshape(nw, capacity, 4 * width)]
    all_to_all x1 -> x0, blocking collectives: 47.5 us -> none  [shards(): lax.all_to_all(returned.astype(jnp.bfloat16), 'wide', split_axis=0, conca...]
    all_gather x2 -> x0, blocking collectives: 37.9 us -> none  [the longest x1 32.5 us: shards(): lax.all_gather(indices, 'wide', axis=0, tiled=True)]
  transfers between devices with their start and end apart: 15 -> 48, of which waited for: 5 -> 21; matrix products, arithmetic and copies ran while one was open for 44% -> 10% of each run, Pallas kernels for 0% -> 9%
where the time goes in v1:
time: 496 us; the launch traced here: 488 us
  waiting for transfers between devices  163 us (33%)
  Pallas kernels  122 us (25%)
  starting transfers between devices  101 us (20%)
  blocking collectives  40.6 us (8%)
  other arithmetic  27.8 us (6%)
  local copies, waits for them, and re-layouts  18.7 us (4%)
  matrix products  12.3 us (2%)
    ppermute x19, waiting for transfers between devices, send(): return lax.ppermute(value, 'dp', [(i, i ^ flip) for i in range(self.nd)])  106 us
    ppermute x26, starting transfers between devices, send(): return lax.ppermute(value, 'wide', [(i, i ^ flip) for i in range(self.nw)])  69.5 us
    ppermute x26, waiting for transfers between devices, send(): return lax.ppermute(value, 'wide', [(i, i ^ flip) for i in range(self.nw)])  56 us
    pallas_call x1, Pallas kernels, ff_call(): pl.pallas_call(lambda *refs: ff_kernel(nd, rows, tile, *refs), grid=(nd,)...  52.5 us
    psum x1, blocking collectives, shards(): lax.psum(jnp.concatenate([dgain_one[0], dgain_two[0], bucket_sums.reshape...  40.6 us
    pallas_call x1, Pallas kernels, attn_back_call(): pl.pallas_call(lambda *refs: attn_back_kernel(nd, rows, batch, *refs), gr...  23.9 us
    pallas_call x1, Pallas kernels, attn_call(): pl.pallas_call(lambda *refs: attn_kernel(nd, rows, batch, *refs), grid=(c...  14.7 us
    ppermute x19, starting transfers between devices, send(): return lax.ppermute(value, 'dp', [(i, i ^ flip) for i in range(self.nd)])  13.7 us
  transfers between devices with their start and end apart: 48, of which 21 were waited for; matrix products, arithmetic and copies ran while one was open for 10% of the time, Pallas kernels for 9%

profile of v1, /device:TPU:0, one launch (start us, length us, event | category | flops | bytes accessed | tf_op | source)
XLA Modules:
  0.0 488.0 jit_solution(6659331271323438674)
XLA Ops:
  2.7 7.3 %all-to-all-start = ((s32[8,1,128]{2,1,0:T(1,128)}), s32[8,1,128]{2,1,0:T(1,128)S(1)}, u32[]{:S(2)}, u32[]{:S(2)}) async-start(s32[8,1,128]{2,1,0:T(1,128)} %bitcast.3), calls=%async_computation | async-start | bytes 8192 | tf_op jit(solution)/shard_map/all_to_all | solution.py:646
  16.4 4.1 convolution_convert_fusion.2
  21.8 5.6 %all-to-all-start.1 = ((bf16[8,21,3072]{2,1,0:T(8,128)(2,1)}), bf16[8,21,3072]{2,1,0:T(8,128)(2,1)S(1)}, u32[]{:S(2)}, u32[]{:S(2)}) async-start(bf16[8,21,3072]{2,1,0:T(8,128)(2,1)} %reshape.359), calls=%async_computation.1 | async-start | bytes 2359296 | tf_op jit(solution)/shard_map/all_to_all | solution.py:660
  28.9 12.8 %collective-permute-done.1.refs_5_.refs_11_.refs_12_.refs_9_ = bf16[784,768]{1,0:T(8,128)(2,1)} collective-permute-done((bf16[784,768]{1,0:T(8,128)(2,1)S(1)}, bf16[784,768]{1,0:T(8,128)(2,1)}, u32[]{:S(2)}, u32[]{:S(2)}) %collective-permute-start.1) | collective-permute-done | bytes 1204256 | tf_op jit(solution)/shard_map/ppermute | solution.py:530
  43.3 2.1 slice_select_fusion
  45.4 10.3 %collective-permute-done.4 = bf16[96,3072]{1,0:T(8,128)(2,1)} collective-permute-done((bf16[96,3072]{1,0:T(8,128)(2,1)S(1)}, bf16[96,3072]{1,0:T(8,128)(2,1)}, u32[]{:S(2)}, u32[]{:S(2)}) %collective-permute-start.4) | collective-permute-done | bytes 589856 | tf_op jit(solution)/shard_map/ppermute | solution.py:530
  59.7 1.9 convolution_convert_fusion.refs_5_.refs_9_
  61.5 7.4 %collective-permute-done.5 = bf16[96,3072]{1,0:T(8,128)(2,1)} collective-permute-done((bf16[96,3072]{1,0:T(8,128)(2,1)}, bf16[96,3072]{1,0:T(8,128)(2,1)}, u32[]{:S(2)}, u32[]{:S(2)}) %collective-permute-start.5) | collective-permute-done | bytes 589856 | tf_op jit(solution)/shard_map/ppermute | solution.py:532
  73.0 13.5 %collective-permute-done.8 = bf16[384,768]{1,0:T(8,128)(2,1)} collective-permute-done((bf16[384,768]{1,0:T(8,128)(2,1)}, bf16[384,768]{1,0:T(8,128)(2,1)}, u32[]{:S(2)}, u32[]{:S(2)}) %collective-permute-start.8) | collective-permute-done | bytes 589856 | tf_op jit(solution)/shard_map/ppermute | solution.py:530
  89.3 12.5 %collective-permute-done.9 = bf16[384,768]{1,0:T(8,128)(2,1)} collective-permute-done((bf16[384,768]{1,0:T(8,128)(2,1)}, bf16[384,768]{1,0:T(8,128)(2,1)}, u32[]{:S(2)}, u32[]{:S(2)}) %collective-permute-start.9) | collective-permute-done | bytes 589856 | tf_op jit(solution)/shard_map/ppermute | solution.py:532
  105.4 8.6 %norm_qkv.1 = (bf16[1024,768]{1,0:T(8,128)(2,1)}, bf16[1024,768]{1,0:T(8,128)(2,1)}, bf16[1024,768]{1,0:T(8,128)(2,1)}, bf16[1024,768]{1,0:T(8,128)(2,1)}) custom-call(s32[1]{0:T(128)} %bitcast.refs_0_, bf16[1024,768]{1,0:T(8,128)(2,1)} %refs_1_.7, f32[1,768]{1,0:T(1,128)} %reshape.357.refs_2_, bf16[784,768]{1,0:T(8,128)(2,1)} %copy-done.3, ...), custom_call_target="tpu_custom_call" | custom-call | flops 3623878656 | bytes 11403264 | tf_op jit(solution)/shard_map/norm_qkv/pallas_call | solution.py:114
  114.0 14.7 %attention.1 = (bf16[16,768,128]{2,1,0:T(8,128)(2,1)}, bf16[1024,768]{1,0:T(8,128)(2,1)}, f32[1024,768]{1,0:T(8,128)}, bf16[1024,768]{1,0:T(8,128)(2,1)}) custom-call(s32[1]{0:T(128)} %bitcast.refs_0_, s32[16]{0:T(128)} %refs_1_.5, bf16[1024,768]{1,0:T(8,128)(2,1)} %get-tuple-element.40.refs_2_.refs_6_, bf16[1024,768]{1,0:T(8,128)(2,1)} %get-tuple-element.41.refs_3_.refs_7_, ...), custom_call_target="tpu_custom_call" | custom-call | flops 7247757312 | bytes 15728640 | tf_op jit(solution)/shard_map/attention/pallas_call | solution.py:202
  128.8 52.5 %feed_forward.1 = (bf16[1024,768]{1,0:T(8,128)(2,1)}, f32[1024,768]{1,0:T(8,128)}, bf16[2,768,768]{2,1,0:T(8,128)(2,1)}, bf16[2,768,768]{2,1,0:T(8,128)(2,1)}, b...) custom-call(s32[1]{0:T(128)} %bitcast.refs_0_, bf16[1024,768]{1,0:T(8,128)(2,1)} %get-tuple-element.43.refs_1_, ...), custom_call_target="tpu_custom_call" | custom-call | flops 28991029248 | bytes 31457280 | tf_op jit(solution)/shard_map/feed_forward/pallas_call | solution.py:313
  181.3 23.9 %attention_back.1 = (f32[1024,768]{1,0:T(8,128)}, bf16[1024,768]{1,0:T(8,128)(2,1)}, bf16[1024,768]{1,0:T(8,128)(2,1)}, bf16[1024,768]{1,0:T(8,128)(2,1)}, bf16[...) custom-call(s32[1]{0:T(128)} %bitcast.refs_0_, ...), custom_call_target="tpu_custom_call" | custom-call | flops 12079595520 | bytes 23592960 | tf_op jit(solution)/shard_map/attention_back/pallas_call | solution.py:415
  205.3 2.0 convolution_convert_fusion.1
  208.6 5.5 %all-to-all-start.2 = ((bf16[8,21,3072]{2,1,0:T(8,128)(2,1)}), bf16[8,21,3072]{2,1,0:T(8,128)(2,1)S(1)}, u32[]{:S(2)}, u32[]{:S(2)}) async-start(bf16[8,21,3072]{2,1,0:T(8,128)(2,1)} %reshape.366), calls=%async_computation.2 | async-start | bytes 2359296 | tf_op jit(solution)/shard_map/all_to_all | solution.py:705
  216.9 2.0 collective-permute-done.42
  219.1 11.2 %square_grads.1 = (bf16[2,768,768]{2,1,0:T(8,128)(2,1)}, bf16[2,768,768]{2,1,0:T(8,128)(2,1)}) custom-call(s32[1]{0:T(128)} %bitcast.refs_0_, bf16[1024,768]{1,0:T(8,128)(2,1)} %get-tuple-element.55.refs_1_, bf16[1024,768]{1,0:T(8,128)(2,1)} %get-tuple-element.56.refs_2_, bf16[1024,768]{1,0:T(8,128)(2,1)} %get-tuple-element.51.refs_4_.refs_3_, ...), custom_call_target="tpu_custom_call" | custom-call | flops 4831838208 | bytes 14155776 | tf_op jit(solution)/shard_map/square_grads/pallas_call | solution.py:455
  230.8 10.9 %input_grad.1 = (f32[1024,768]{1,0:T(8,128)}, f32[1,768]{1,0:T(1,128)}) custom-call(s32[1]{0:T(128)} %bitcast.refs_0_, bf16[1024,768]{1,0:T(8,128)(2,1)} %refs_1_.7, f32[1,768]{1,0:T(1,128)} %reshape.357.refs_2_, f32[1024,768]{1,0:T(8,128)} %get-tuple-element.50.refs_3_, bf16[1024,768]{1,0:T(8,128)(2,1)} %get-tuple-element.51.refs_4_.refs_3_, ...), custom_call_target="tpu_custom_call" | custom-call | flops 3623878656 | bytes 16121856 | tf_op jit(solution)/shard_map/input_grad/pallas_call | solution.py:497
  243.0 2.9 broadcast_select_fusion.7
  248.3 40.6 %psum.7 = f32[1920]{0:T(1024)S(1)} all-reduce(f32[1920]{0:T(1024)S(1)} %pad_maximum_fusion.8), channel_id=1, replica_groups=mesh['dp'=4,'wide'=8] {'dp','wide'}, use_global_device_ids=true, to_apply=%region_2.3 | all-reduce | flops 1920 | bytes 15360 | tf_op jit(solution)/shard_map/psum | solution.py:723
  291.0 2.4 collective-permute-start.44
  293.4 1.8 fusion.2
  296.7 1.8 fusion.3
  302.3 3.8 collective-permute-done.44
  306.1 3.2 fusion
  309.3 22.1 %collective-permute-done.12 = bf16[768,768]{1,0:T(8,128)(2,1)S(1)} collective-permute-done((bf16[768,768]{1,0:T(8,128)(2,1)S(1)}, bf16[768,768]{1,0:T(8,128)(2,1)S(1)}, u32[]{:S(2)}, u32[]{:S(2)}) %collective-permute-start.12) | collective-permute-done | bytes 1179680 | tf_op jit(solution)/shard_map/ppermute | solution.py:530
  333.1 2.1 collective-permute-start.13
  335.2 21.5 %collective-permute-done.22 = bf16[192,3072]{1,0:T(8,128)(2,1)S(1)} collective-permute-done((bf16[192,3072]{1,0:T(8,128)(2,1)S(1)}, bf16[192,3072]{1,0:T(8,128)(2,1)S(1)}, u32[]{:S(2)}, u32[]{:S(2)}) %collective-permute-start.22) | collective-permute-done | bytes 1179680 | tf_op jit(solution)/shard_map/ppermute | solution.py:530
  356.6 1.8 bitcast_add_fusion.1
  358.6 2.1 collective-permute-start.23
  360.6 19.0 %collective-permute-done.32 = bf16[768,768]{1,0:T(8,128)(2,1)S(1)} collective-permute-done((bf16[768,768]{1,0:T(8,128)(2,1)S(1)}, bf16[768,768]{1,0:T(8,128)(2,1)S(1)}, u32[]{:S(2)}, u32[]{:S(2)}) %collective-permute-start.32) | collective-permute-done | bytes 1179680 | tf_op jit(solution)/shard_map/ppermute | solution.py:530
  388.4 6.1 %collective-permute-done.33 = bf16[768,384]{1,0:T(8,128)(2,1)S(1)} collective-permute-done((bf16[768,384]{1,0:T(8,128)(2,1)S(1)}, bf16[768,384]{1,0:T(8,128)(2,1)S(1)}, u32[]{:S(2)}, u32[]{:S(2)}) %collective-permute-start.33) | collective-permute-done | bytes 589856 | tf_op jit(solution)/shard_map/ppermute | solution.py:532
  394.5 2.3 collective-permute-start.25
  398.8 10.3 %collective-permute-start.35 = (bf16[192,384]{1,0:T(8,128)(2,1)S(1)}, bf16[192,384]{1,0:T(8,128)(2,1)S(1)}, u32[]{:S(2)}, u32[]{:S(2)}) collective-permute-start(bf16[192,384]{1,0:T(8,128)(2,1)S(1)} %get-tuple-element.77), channel_id=1, source_target_pairs={{0,4},{1,5},{2,6},{3,7},{4,0},{5,1},{6,2},{7,3},{8,12},{9,13},{10,... | collective-permute-start | bytes 442376 | tf_op jit(solution)/shard_map/ppermute | solution.py:532
  410.1 2.4 collective-permute-done.25
  412.5 9.7 %collective-permute-start.18 = (bf16[192,384]{1,0:T(8,128)(2,1)S(1)}, bf16[192,384]{1,0:T(8,128)(2,1)S(1)}, u32[]{:S(2)}, u32[]{:S(2)}) collective-permute-start(bf16[192,384]{1,0:T(8,128)(2,1)S(1)} %add_convert_fusion.5), channel_id=1, source_target_pairs={{0,4},{1,5},{2,6},{3,7},{4,0},{5,1},{6,2},{7,3},{8,12},{9,13},{10,... | collective-permute-start | bytes 442376 | tf_op jit(solution)/shard_map/ppermute | solution.py:532
  422.3 1.9 collective-permute-start.17
  424.3 9.3 %collective-permute-start.28 = (bf16[48,1536]{1,0:T(8,128)(2,1)S(1)}, bf16[48,1536]{1,0:T(8,128)(2,1)S(1)}, u32[]{:S(2)}, u32[]{:S(2)}) collective-permute-start(bf16[48,1536]{1,0:T(8,128)(2,1)S(1)} %add_convert_fusion.4), channel_id=1, source_target_pairs={{0,4},{1,5},{2,6},{3,7},{4,0},{5,1},{6,2},{7,3},{8,12},{9,13},{10,... | collective-permute-start | bytes 442376 | tf_op jit(solution)/shard_map/ppermute | solution.py:532
  433.7 3.0 collective-permute-start.27
  436.9 8.3 %collective-permute-start.38 = (bf16[192,384]{1,0:T(8,128)(2,1)S(1)}, bf16[192,384]{1,0:T(8,128)(2,1)S(1)}, u32[]{:S(2)}, u32[]{:S(2)}) collective-permute-start(bf16[192,384]{1,0:T(8,128)(2,1)S(1)} %add_convert_fusion.3), channel_id=1, source_target_pairs={{0,4},{1,5},{2,6},{3,7},{4,0},{5,1},{6,2},{7,3},{8,12},{9,13},{10,... | collective-permute-start | bytes 442376 | tf_op jit(solution)/shard_map/ppermute | solution.py:532
  445.4 3.2 collective-permute-start.37
  449.6 4.5 collective-permute-start.20
  454.2 4.8 collective-permute-done.38
  460.5 7.7 %collective-permute-done.20 = bf16[768,384]{1,0:T(8,128)(2,1)S(1)} collective-permute-done((bf16[768,384]{1,0:T(8,128)(2,1)S(1)}, bf16[768,384]{1,0:T(8,128)(2,1)S(1)}, u32[]{:S(2)}, u32[]{:S(2)}) %collective-permute-start.20) | collective-permute-done | bytes 589856 | tf_op jit(solution)/shard_map/ppermute | solution.py:532
  468.7 10.7 %collective-permute-done.30 = bf16[192,1536]{1,0:T(8,128)(2,1)S(1)} collective-permute-done((bf16[192,1536]{1,0:T(8,128)(2,1)S(1)}, bf16[192,1536]{1,0:T(8,128)(2,1)S(1)}, u32[]{:S(2)}, u32[]{:S(2)}) %collective-permute-start.30) | collective-permute-done | bytes 589856 | tf_op jit(solution)/shard_map/ppermute | solution.py:532
  481.1 1.7 maximum_convert_fusion.1
  482.7 3.0 collective-permute-done.40
  (195 shorter events, 63.5 us)
Async XLA Ops:
  2.7 13.6 %all-to-all-start = ((s32[8,1,128]{2,1,0:T(1,128)}), s32[8,1,128]{2,1,0:T(1,128)S(1)}, u32[]{:S(2)}, u32[]{:S(2)}) async-start(s32[8,1,128]{2,1,0:T(1,128)} %bitcast.3), calls=%async_computation | async-start | bytes 8192 | tf_op jit(solution)/shard_map/all_to_all | solution.py:646
  13.6 28.1 %collective-permute-start.1 = (bf16[784,768]{1,0:T(8,128)(2,1)S(1)}, bf16[784,768]{1,0:T(8,128)(2,1)}, u32[]{:S(2)}, u32[]{:S(2)}) collective-permute-start(bf16[784,768]{1,0:T(8,128)(2,1)S(1)} %constant_dynamic-update-slice_fusion.refs_3_.refs_9_.refs_10_.refs_7_), channel_id=1, source_target_pairs={{0,16},{8,24},{16,0},{24,8},{1,17},{9,25},{17,1},{25,9},{2,18},{10... | collective-permute-start | bytes 3612680 | tf_op jit(solution)/shard_map/ppermute | solution.py:530
  15.2 42.8 %collective-permute-start = (bf16[784,768]{1,0:T(8,128)(2,1)S(1)}, bf16[784,768]{1,0:T(8,128)(2,1)}, u32[]{:S(2)}, u32[]{:S(2)}) collective-permute-start(bf16[784,768]{1,0:T(8,128)(2,1)S(1)} %constant_dynamic-update-slice_fusion.refs_3_.refs_9_.refs_10_.refs_7_), channel_id=1, source_target_pairs={{0,8},{8,0},{16,24},{24,16},{1,9},{9,1},{17,25},{25,17},{2,10},{10... | collective-permute-start | bytes 3612680 | tf_op jit(solution)/shard_map/ppermute | solution.py:530
  15.2 113.6 %collective-permute-start.3 = (bf16[192,3072]{1,0:T(8,128)(2,1)}, bf16[192,3072]{1,0:T(8,128)(2,1)}, u32[]{:S(2)}, u32[]{:S(2)}) collective-permute-start(bf16[192,3072]{1,0:T(8,128)(2,1)} %refs_4_.1), channel_id=1, source_target_pairs={{0,8},{8,0},{16,24},{24,16},{1,9},{9,1},{17,25},{25,17},{2,10},{10... | collective-permute-start | bytes 3538952 | tf_op jit(solution)/shard_map/ppermute | solution.py:530
  15.7 113.1 %collective-permute-start.7 = (bf16[768,768]{1,0:T(8,128)(2,1)}, bf16[768,768]{1,0:T(8,128)(2,1)}, u32[]{:S(2)}, u32[]{:S(2)}) collective-permute-start(bf16[768,768]{1,0:T(8,128)(2,1)} %refs_8_.1), channel_id=1, source_target_pairs={{0,8},{8,0},{16,24},{24,16},{1,9},{9,1},{17,25},{25,17},{2,10},{10... | collective-permute-start | bytes 3538952 | tf_op jit(solution)/shard_map/ppermute | solution.py:530
  21.8 37.5 %all-to-all-start.1 = ((bf16[8,21,3072]{2,1,0:T(8,128)(2,1)}), bf16[8,21,3072]{2,1,0:T(8,128)(2,1)S(1)}, u32[]{:S(2)}, u32[]{:S(2)}) async-start(bf16[8,21,3072]{2,1,0:T(8,128)(2,1)} %reshape.359), calls=%async_computation.1 | async-start | bytes 2359296 | tf_op jit(solution)/shard_map/all_to_all | solution.py:660
  41.7 14.0 %collective-permute-start.4 = (bf16[96,3072]{1,0:T(8,128)(2,1)S(1)}, bf16[96,3072]{1,0:T(8,128)(2,1)}, u32[]{:S(2)}, u32[]{:S(2)}) collective-permute-start(bf16[96,3072]{1,0:T(8,128)(2,1)S(1)} %slice_select_fusion.1), channel_id=1, source_target_pairs={{0,16},{8,24},{16,0},{24,8},{1,17},{9,25},{17,1},{25,9},{2,18},{10... | collective-permute-start | bytes 1769480 | tf_op jit(solution)/shard_map/ppermute | solution.py:530
  55.7 13.3 %collective-permute-start.5 = (bf16[96,3072]{1,0:T(8,128)(2,1)}, bf16[96,3072]{1,0:T(8,128)(2,1)}, u32[]{:S(2)}, u32[]{:S(2)}) collective-permute-start(bf16[96,3072]{1,0:T(8,128)(2,1)} %collective-permute-done.4), channel_id=1, source_target_pairs={{0,1},{1,0},{2,3},{3,2},{4,5},{5,4},{6,7},{7,6},{8,9},{9,8},{10,11... | collective-permute-start | bytes 1769480 | tf_op jit(solution)/shard_map/ppermute | solution.py:532
  59.3 12.7 %collective-permute-start.2 = (bf16[784,768]{1,0:T(8,128)(2,1)}, bf16[784,768]{1,0:T(8,128)(2,1)S(1)}, u32[]{:S(2)}, u32[]{:S(2)}) collective-permute-start(bf16[784,768]{1,0:T(8,128)(2,1)} %collective-permute-done.1.refs_5_.refs_11_.refs_12_.refs_9_), channel_id=1, source_target_pairs={{0,8},{8,0},{16,24},{24,16},{1,9},{9,1},{17,25},{25,17},{2,10},{10... | collective-permute-start | bytes 3612680 | tf_op jit(solution)/shard_map/ppermute | solution.py:530
  70.4 58.4 %collective-permute-start.6 = (bf16[192,3072]{1,0:T(8,128)(2,1)S(1)}, bf16[192,3072]{1,0:T(8,128)(2,1)}, u32[]{:S(2)}, u32[]{:S(2)}) collective-permute-start(bf16[192,3072]{1,0:T(8,128)(2,1)S(1)} %pad_maximum_fusion.refs_6_), channel_id=1, source_target_pairs={{0,8},{8,0},{16,24},{24,16},{1,9},{9,1},{17,25},{25,17},{2,10},{10... | collective-permute-start | bytes 3538952 | tf_op jit(solution)/shard_map/ppermute | solution.py:530
  70.5 16.1 %collective-permute-start.8 = (bf16[384,768]{1,0:T(8,128)(2,1)}, bf16[384,768]{1,0:T(8,128)(2,1)}, u32[]{:S(2)}, u32[]{:S(2)}) collective-permute-start(bf16[384,768]{1,0:T(8,128)(2,1)} %slice_select_fusion), channel_id=1, source_target_pairs={{0,16},{8,24},{16,0},{24,8},{1,17},{9,25},{17,1},{25,9},{2,18},{10... | collective-permute-start | bytes 1769480 | tf_op jit(solution)/shard_map/ppermute | solution.py:530
  86.5 15.2 %collective-permute-start.9 = (bf16[384,768]{1,0:T(8,128)(2,1)}, bf16[384,768]{1,0:T(8,128)(2,1)}, u32[]{:S(2)}, u32[]{:S(2)}) collective-permute-start(bf16[384,768]{1,0:T(8,128)(2,1)} %collective-permute-done.8), channel_id=1, source_target_pairs={{0,1},{1,0},{2,3},{3,2},{4,5},{5,4},{6,7},{7,6},{8,9},{9,8},{10,11... | collective-permute-start | bytes 1769480 | tf_op jit(solution)/shard_map/ppermute | solution.py:532
  103.2 25.6 %collective-permute-start.10 = (bf16[768,768]{1,0:T(8,128)(2,1)S(1)}, bf16[768,768]{1,0:T(8,128)(2,1)}, u32[]{:S(2)}, u32[]{:S(2)}) collective-permute-start(bf16[768,768]{1,0:T(8,128)(2,1)S(1)} %pad_maximum_fusion.1.refs_10_), channel_id=1, source_target_pairs={{0,8},{8,0},{16,24},{24,16},{1,9},{9,1},{17,25},{25,17},{2,10},{10... | collective-permute-start | bytes 3538952 | tf_op jit(solution)/shard_map/ppermute | solution.py:530
  208.6 33.8 %all-to-all-start.2 = ((bf16[8,21,3072]{2,1,0:T(8,128)(2,1)}), bf16[8,21,3072]{2,1,0:T(8,128)(2,1)S(1)}, u32[]{:S(2)}, u32[]{:S(2)}) async-start(bf16[8,21,3072]{2,1,0:T(8,128)(2,1)} %reshape.366), calls=%async_computation.2 | async-start | bytes 2359296 | tf_op jit(solution)/shard_map/all_to_all | solution.py:705
  214.1 1.2 collective-permute-start.41
  215.3 3.7 collective-permute-start.42
  230.3 63.1 %collective-permute-start.11 = (bf16[2,768,768]{2,1,0:T(8,128)(2,1)}, bf16[2,768,768]{2,1,0:T(8,128)(2,1)}, u32[]{:S(2)}, u32[]{:S(2)}) collective-permute-start(bf16[2,768,768]{2,1,0:T(8,128)(2,1)} %get-tuple-element.59), channel_id=1, source_target_pairs={{0,8},{8,0},{16,24},{24,16},{1,9},{9,1},{17,25},{25,17},{2,10},{10... | collective-permute-start | bytes 7077896 | tf_op jit(solution)/shard_map/ppermute | solution.py:530
  230.3 66.4 %collective-permute-start.21 = (bf16[2,192,3072]{2,1,0:T(8,128)(2,1)}, bf16[2,192,3072]{2,1,0:T(8,128)(2,1)}, u32[]{:S(2)}, u32[]{:S(2)}) collective-permute-start(bf16[2,192,3072]{2,1,0:T(8,128)(2,1)} %get-tuple-element.61), channel_id=1, source_target_pairs={{0,8},{8,0},{16,24},{24,16},{1,9},{9,1},{17,25},{25,17},{2,10},{10... | collective-permute-start | bytes 7077896 | tf_op jit(solution)/shard_map/ppermute | solution.py:530
  230.8 68.3 %collective-permute-start.31 = (bf16[2,768,768]{2,1,0:T(8,128)(2,1)}, bf16[2,768,768]{2,1,0:T(8,128)(2,1)}, u32[]{:S(2)}, u32[]{:S(2)}) collective-permute-start(bf16[2,768,768]{2,1,0:T(8,128)(2,1)} %get-tuple-element.63), channel_id=1, source_target_pairs={{0,8},{8,0},{16,24},{24,16},{1,9},{9,1},{17,25},{25,17},{2,10},{10... | collective-permute-start | bytes 7077896 | tf_op jit(solution)/shard_map/ppermute | solution.py:530
  246.1 44.8 %collective-permute-start.43 = (bf16[2,168,768]{2,1,0:T(8,128)(2,1)S(1)}, bf16[2,168,768]{2,1,0:T(8,128)(2,1)S(1)}, u32[]{:S(2)}, u32[]{:S(2)}) collective-permute-start(bf16[2,168,768]{2,1,0:T(8,128)(2,1)S(1)} %pad_maximum_fusion.5), channel_id=1, source_target_pairs={{0,8},{8,0},{16,24},{24,16},{1,9},{9,1},{17,25},{25,17},{2,10},{10... | collective-permute-start | bytes 1548296 | tf_op jit(solution)/shard_map/ppermute | solution.py:530
  291.0 15.0 %collective-permute-start.44 = (bf16[336,768]{1,0:T(8,128)(2,1)S(1)}, bf16[336,768]{1,0:T(8,128)(2,1)S(1)}, u32[]{:S(2)}, u32[]{:S(2)}) collective-permute-start(bf16[336,768]{1,0:T(8,128)(2,1)S(1)} %pad_maximum_fusion.6), channel_id=1, source_target_pairs={{0,16},{8,24},{16,0},{24,8},{1,17},{9,25},{17,1},{25,9},{2,18},{10... | collective-permute-start | bytes 1548296 | tf_op jit(solution)/shard_map/ppermute | solution.py:530
  295.2 36.2 %collective-permute-start.12 = (bf16[768,768]{1,0:T(8,128)(2,1)S(1)}, bf16[768,768]{1,0:T(8,128)(2,1)S(1)}, u32[]{:S(2)}, u32[]{:S(2)}) collective-permute-start(bf16[768,768]{1,0:T(8,128)(2,1)S(1)} %fusion.2), channel_id=1, source_target_pairs={{0,16},{8,24},{16,0},{24,8},{1,17},{9,25},{17,1},{25,9},{2,18},{10... | collective-permute-start | bytes 3538952 | tf_op jit(solution)/shard_map/ppermute | solution.py:530
  298.5 58.1 %collective-permute-start.22 = (bf16[192,3072]{1,0:T(8,128)(2,1)S(1)}, bf16[192,3072]{1,0:T(8,128)(2,1)S(1)}, u32[]{:S(2)}, u32[]{:S(2)}) collective-permute-start(bf16[192,3072]{1,0:T(8,128)(2,1)S(1)} %fusion.3), channel_id=1, source_target_pairs={{0,16},{8,24},{16,0},{24,8},{1,17},{9,25},{17,1},{25,9},{2,18},{10... | collective-permute-start | bytes 3538952 | tf_op jit(solution)/shard_map/ppermute | solution.py:530
  300.8 78.8 %collective-permute-start.32 = (bf16[768,768]{1,0:T(8,128)(2,1)S(1)}, bf16[768,768]{1,0:T(8,128)(2,1)S(1)}, u32[]{:S(2)}, u32[]{:S(2)}) collective-permute-start(bf16[768,768]{1,0:T(8,128)(2,1)S(1)} %fusion.4), channel_id=1, source_target_pairs={{0,16},{8,24},{16,0},{24,8},{1,17},{9,25},{17,1},{25,9},{2,18},{10... | collective-permute-start | bytes 3538952 | tf_op jit(solution)/shard_map/ppermute | solution.py:530
  333.1 49.7 %collective-permute-start.13 = (bf16[768,384]{1,0:T(8,128)(2,1)S(1)}, bf16[768,384]{1,0:T(8,128)(2,1)S(1)}, u32[]{:S(2)}, u32[]{:S(2)}) collective-permute-start(bf16[768,384]{1,0:T(8,128)(2,1)S(1)} %select_convert_fusion.2), channel_id=1, source_target_pairs={{0,1},{1,0},{2,3},{3,2},{4,5},{5,4},{6,7},{7,6},{8,9},{9,8},{10,11... | collective-permute-start | bytes 1769480 | tf_op jit(solution)/shard_map/ppermute | solution.py:532
  358.6 28.9 %collective-permute-start.23 = (bf16[192,1536]{1,0:T(8,128)(2,1)S(1)}, bf16[192,1536]{1,0:T(8,128)(2,1)S(1)}, u32[]{:S(2)}, u32[]{:S(2)}) collective-permute-start(bf16[192,1536]{1,0:T(8,128)(2,1)S(1)} %select_convert_fusion.1), channel_id=1, source_target_pairs={{0,1},{1,0},{2,3},{3,2},{4,5},{5,4},{6,7},{7,6},{8,9},{9,8},{10,11... | collective-permute-start | bytes 1769480 | tf_op jit(solution)/shard_map/ppermute | solution.py:532
  381.4 13.1 %collective-permute-start.33 = (bf16[768,384]{1,0:T(8,128)(2,1)S(1)}, bf16[768,384]{1,0:T(8,128)(2,1)S(1)}, u32[]{:S(2)}, u32[]{:S(2)}) collective-permute-start(bf16[768,384]{1,0:T(8,128)(2,1)S(1)} %select_convert_fusion), channel_id=1, source_target_pairs={{0,1},{1,0},{2,3},{3,2},{4,5},{5,4},{6,7},{7,6},{8,9},{9,8},{10,11... | collective-permute-start | bytes 1769480 | tf_op jit(solution)/shard_map/ppermute | solution.py:532
  383.0 14.1 %collective-permute-start.14 = (bf16[192,384]{1,0:T(8,128)(2,1)S(1)}, bf16[192,384]{1,0:T(8,128)(2,1)S(1)}, u32[]{:S(2)}, u32[]{:S(2)}) collective-permute-start(bf16[192,384]{1,0:T(8,128)(2,1)S(1)} %get-tuple-element.86), channel_id=1, source_target_pairs={{0,2},{1,3},{2,0},{3,1},{4,6},{5,7},{6,4},{7,5},{8,10},{9,11},{10,... | collective-permute-start | bytes 442376 | tf_op jit(solution)/shard_map/ppermute | solution.py:532
  384.6 14.2 %collective-permute-start.15 = (bf16[192,384]{1,0:T(8,128)(2,1)S(1)}, bf16[192,384]{1,0:T(8,128)(2,1)S(1)}, u32[]{:S(2)}, u32[]{:S(2)}) collective-permute-start(bf16[192,384]{1,0:T(8,128)(2,1)S(1)} %get-tuple-element.87), channel_id=1, source_target_pairs={{0,4},{1,5},{2,6},{3,7},{4,0},{5,1},{6,2},{7,3},{8,12},{9,13},{10,... | collective-permute-start | bytes 442376 | tf_op jit(solution)/shard_map/ppermute | solution.py:532
  385.9 12.9 %collective-permute-start.16 = (bf16[192,384]{1,0:T(8,128)(2,1)S(1)}, bf16[192,384]{1,0:T(8,128)(2,1)S(1)}, u32[]{:S(2)}, u32[]{:S(2)}) collective-permute-start(bf16[192,384]{1,0:T(8,128)(2,1)S(1)} %get-tuple-element.88), channel_id=1, source_target_pairs={{0,6},{1,7},{2,4},{3,5},{4,2},{5,3},{6,0},{7,1},{8,14},{9,15},{10,... | collective-permute-start | bytes 442376 | tf_op jit(solution)/shard_map/ppermute | solution.py:532
  387.8 21.4 %collective-permute-start.24 = (bf16[48,1536]{1,0:T(8,128)(2,1)S(1)}, bf16[48,1536]{1,0:T(8,128)(2,1)S(1)}, u32[]{:S(2)}, u32[]{:S(2)}) collective-permute-start(bf16[48,1536]{1,0:T(8,128)(2,1)S(1)} %get-tuple-element.81), channel_id=1, source_target_pairs={{0,2},{1,3},{2,0},{3,1},{4,6},{5,7},{6,4},{7,5},{8,10},{9,11},{10,... | collective-permute-start | bytes 442376 | tf_op jit(solution)/shard_map/ppermute | solution.py:532
  394.5 18.0 %collective-permute-start.25 = (bf16[48,1536]{1,0:T(8,128)(2,1)S(1)}, bf16[48,1536]{1,0:T(8,128)(2,1)S(1)}, u32[]{:S(2)}, u32[]{:S(2)}) collective-permute-start(bf16[48,1536]{1,0:T(8,128)(2,1)S(1)} %get-tuple-element.82), channel_id=1, source_target_pairs={{0,4},{1,5},{2,6},{3,7},{4,0},{5,1},{6,2},{7,3},{8,12},{9,13},{10,... | collective-permute-start | bytes 442376 | tf_op jit(solution)/shard_map/ppermute | solution.py:532
  397.2 15.3 %collective-permute-start.26 = (bf16[48,1536]{1,0:T(8,128)(2,1)S(1)}, bf16[48,1536]{1,0:T(8,128)(2,1)S(1)}, u32[]{:S(2)}, u32[]{:S(2)}) collective-permute-start(bf16[48,1536]{1,0:T(8,128)(2,1)S(1)} %get-tuple-element.83), channel_id=1, source_target_pairs={{0,6},{1,7},{2,4},{3,5},{4,2},{5,3},{6,0},{7,1},{8,14},{9,15},{10,... | collective-permute-start | bytes 442376 | tf_op jit(solution)/shard_map/ppermute | solution.py:532
  398.8 23.5 %collective-permute-start.34 = (bf16[192,384]{1,0:T(8,128)(2,1)S(1)}, bf16[192,384]{1,0:T(8,128)(2,1)S(1)}, u32[]{:S(2)}, u32[]{:S(2)}) collective-permute-start(bf16[192,384]{1,0:T(8,128)(2,1)S(1)} %get-tuple-element.76), channel_id=1, source_target_pairs={{0,2},{1,3},{2,0},{3,1},{4,6},{5,7},{6,4},{7,5},{8,10},{9,11},{10,... | collective-permute-start | bytes 442376 | tf_op jit(solution)/shard_map/ppermute | solution.py:532
  398.8 25.5 %collective-permute-start.35 = (bf16[192,384]{1,0:T(8,128)(2,1)S(1)}, bf16[192,384]{1,0:T(8,128)(2,1)S(1)}, u32[]{:S(2)}, u32[]{:S(2)}) collective-permute-start(bf16[192,384]{1,0:T(8,128)(2,1)S(1)} %get-tuple-element.77), channel_id=1, source_target_pairs={{0,4},{1,5},{2,6},{3,7},{4,0},{5,1},{6,2},{7,3},{8,12},{9,13},{10,... | collective-permute-start | bytes 442376 | tf_op jit(solution)/shard_map/ppermute | solution.py:532
  409.2 15.1 %collective-permute-start.36 = (bf16[192,384]{1,0:T(8,128)(2,1)S(1)}, bf16[192,384]{1,0:T(8,128)(2,1)S(1)}, u32[]{:S(2)}, u32[]{:S(2)}) collective-permute-start(bf16[192,384]{1,0:T(8,128)(2,1)S(1)} %get-tuple-element.78), channel_id=1, source_target_pairs={{0,6},{1,7},{2,4},{3,5},{4,2},{5,3},{6,0},{7,1},{8,14},{9,15},{10,... | collective-permute-start | bytes 442376 | tf_op jit(solution)/shard_map/ppermute | solution.py:532
  412.5 21.2 %collective-permute-start.19 = (bf16[192,384]{1,0:T(8,128)(2,1)S(1)}, bf16[192,384]{1,0:T(8,128)(2,1)S(1)}, u32[]{:S(2)}, u32[]{:S(2)}) collective-permute-start(bf16[192,384]{1,0:T(8,128)(2,1)S(1)} %add_convert_fusion.5), channel_id=1, source_target_pairs={{0,2},{1,3},{2,0},{3,1},{4,6},{5,7},{6,4},{7,5},{8,10},{9,11},{10,... | collective-permute-start | bytes 442376 | tf_op jit(solution)/shard_map/ppermute | solution.py:532
  412.5 24.4 %collective-permute-start.18 = (bf16[192,384]{1,0:T(8,128)(2,1)S(1)}, bf16[192,384]{1,0:T(8,128)(2,1)S(1)}, u32[]{:S(2)}, u32[]{:S(2)}) collective-permute-start(bf16[192,384]{1,0:T(8,128)(2,1)S(1)} %add_convert_fusion.5), channel_id=1, source_target_pairs={{0,4},{1,5},{2,6},{3,7},{4,0},{5,1},{6,2},{7,3},{8,12},{9,13},{10,... | collective-permute-start | bytes 442376 | tf_op jit(solution)/shard_map/ppermute | solution.py:532
  422.3 14.6 %collective-permute-start.17 = (bf16[192,384]{1,0:T(8,128)(2,1)S(1)}, bf16[192,384]{1,0:T(8,128)(2,1)S(1)}, u32[]{:S(2)}, u32[]{:S(2)}) collective-permute-start(bf16[192,384]{1,0:T(8,128)(2,1)S(1)} %add_convert_fusion.5), channel_id=1, source_target_pairs={{0,6},{1,7},{2,4},{3,5},{4,2},{5,3},{6,0},{7,1},{8,14},{9,15},{10,... | collective-permute-start | bytes 442376 | tf_op jit(solution)/shard_map/ppermute | solution.py:532
  424.3 21.1 %collective-permute-start.29 = (bf16[48,1536]{1,0:T(8,128)(2,1)S(1)}, bf16[48,1536]{1,0:T(8,128)(2,1)S(1)}, u32[]{:S(2)}, u32[]{:S(2)}) collective-permute-start(bf16[48,1536]{1,0:T(8,128)(2,1)S(1)} %add_convert_fusion.4), channel_id=1, source_target_pairs={{0,2},{1,3},{2,0},{3,1},{4,6},{5,7},{6,4},{7,5},{8,10},{9,11},{10,... | collective-permute-start | bytes 442376 | tf_op jit(solution)/shard_map/ppermute | solution.py:532
  424.3 25.3 %collective-permute-start.28 = (bf16[48,1536]{1,0:T(8,128)(2,1)S(1)}, bf16[48,1536]{1,0:T(8,128)(2,1)S(1)}, u32[]{:S(2)}, u32[]{:S(2)}) collective-permute-start(bf16[48,1536]{1,0:T(8,128)(2,1)S(1)} %add_convert_fusion.4), channel_id=1, source_target_pairs={{0,4},{1,5},{2,6},{3,7},{4,0},{5,1},{6,2},{7,3},{8,12},{9,13},{10,... | collective-permute-start | bytes 442376 | tf_op jit(solution)/shard_map/ppermute | solution.py:532
  433.7 20.4 %collective-permute-start.27 = (bf16[48,1536]{1,0:T(8,128)(2,1)S(1)}, bf16[48,1536]{1,0:T(8,128)(2,1)S(1)}, u32[]{:S(2)}, u32[]{:S(2)}) collective-permute-start(bf16[48,1536]{1,0:T(8,128)(2,1)S(1)} %add_convert_fusion.4), channel_id=1, source_target_pairs={{0,6},{1,7},{2,4},{3,5},{4,2},{5,3},{6,0},{7,1},{8,14},{9,15},{10,... | collective-permute-start | bytes 442376 | tf_op jit(solution)/shard_map/ppermute | solution.py:532
  436.9 17.3 %collective-permute-start.39 = (bf16[192,384]{1,0:T(8,128)(2,1)S(1)}, bf16[192,384]{1,0:T(8,128)(2,1)S(1)}, u32[]{:S(2)}, u32[]{:S(2)}) collective-permute-start(bf16[192,384]{1,0:T(8,128)(2,1)S(1)} %add_convert_fusion.3), channel_id=1, source_target_pairs={{0,2},{1,3},{2,0},{3,1},{4,6},{5,7},{6,4},{7,5},{8,10},{9,11},{10,... | collective-permute-start | bytes 442376 | tf_op jit(solution)/shard_map/ppermute | solution.py:532
  436.9 22.1 %collective-permute-start.38 = (bf16[192,384]{1,0:T(8,128)(2,1)S(1)}, bf16[192,384]{1,0:T(8,128)(2,1)S(1)}, u32[]{:S(2)}, u32[]{:S(2)}) collective-permute-start(bf16[192,384]{1,0:T(8,128)(2,1)S(1)} %add_convert_fusion.3), channel_id=1, source_target_pairs={{0,4},{1,5},{2,6},{3,7},{4,0},{5,1},{6,2},{7,3},{8,12},{9,13},{10,... | collective-permute-start | bytes 442376 | tf_op jit(solution)/shard_map/ppermute | solution.py:532
  445.4 13.7 %collective-permute-start.37 = (bf16[192,384]{1,0:T(8,128)(2,1)S(1)}, bf16[192,384]{1,0:T(8,128)(2,1)S(1)}, u32[]{:S(2)}, u32[]{:S(2)}) collective-permute-start(bf16[192,384]{1,0:T(8,128)(2,1)S(1)} %add_convert_fusion.3), channel_id=1, source_target_pairs={{0,6},{1,7},{2,4},{3,5},{4,2},{5,3},{6,0},{7,1},{8,14},{9,15},{10,... | collective-permute-start | bytes 442376 | tf_op jit(solution)/shard_map/ppermute | solution.py:532
  449.6 18.7 %collective-permute-start.20 = (bf16[768,384]{1,0:T(8,128)(2,1)S(1)}, bf16[768,384]{1,0:T(8,128)(2,1)S(1)}, u32[]{:S(2)}, u32[]{:S(2)}) collective-permute-start(bf16[768,384]{1,0:T(8,128)(2,1)S(1)} %pad_maximum_fusion.2), channel_id=1, source_target_pairs={{0,1},{1,0},{2,3},{3,2},{4,5},{5,4},{6,7},{7,6},{8,9},{9,8},{10,11... | collective-permute-start | bytes 1769480 | tf_op jit(solution)/shard_map/ppermute | solution.py:532
  454.1 25.3 %collective-permute-start.30 = (bf16[192,1536]{1,0:T(8,128)(2,1)S(1)}, bf16[192,1536]{1,0:T(8,128)(2,1)S(1)}, u32[]{:S(2)}, u32[]{:S(2)}) collective-permute-start(bf16[192,1536]{1,0:T(8,128)(2,1)S(1)} %pad_maximum_fusion.3), channel_id=1, source_target_pairs={{0,1},{1,0},{2,3},{3,2},{4,5},{5,4},{6,7},{7,6},{8,9},{9,8},{10,11... | collective-permute-start | bytes 1769480 | tf_op jit(solution)/shard_map/ppermute | solution.py:532
  459.2 26.5 %collective-permute-start.40 = (bf16[768,384]{1,0:T(8,128)(2,1)S(1)}, bf16[768,384]{1,0:T(8,128)(2,1)S(1)}, u32[]{:S(2)}, u32[]{:S(2)}) collective-permute-start(bf16[768,384]{1,0:T(8,128)(2,1)S(1)} %pad_maximum_fusion.4), channel_id=1, source_target_pairs={{0,1},{1,0},{2,3},{3,2},{4,5},{5,4},{6,7},{7,6},{8,9},{9,8},{10,11... | collective-permute-start | bytes 1769480 | tf_op jit(solution)/shard_map/ppermute | solution.py:532
  (16 other events, 139.9 us)
